TPU v7x, 512 devices: a whole 4x8x8 slice. The times are simulated.
512 devices in a mesh: blk: 64 (over z, x, y_lo), head: 8 (over y_hi, core).
Axes of the slice: x: 4, y: 8 (y_hi: 4, y_lo: 2; y = y_hi * 2 + y_lo), z: 8, core: 2. Of those that a mesh axis runs over, the one named last changes fastest.
Arguments:
- queries: bfloat16 [65536, 2048], P('blk', 'head'), parts along dimension 1, may hold values from -6 to 6
- outputs: bfloat16 [65536, 2048], P('blk', 'head'), parts along dimension 1, may hold values from -6 to 6
- out_grads: bfloat16 [65536, 2048], P('blk', 'head'), parts along dimension 1, may hold values from -9 to 9
- log_sums: float32 [32, 65536], P('head', 'blk'), parts along dimension 0, may hold values from 4.5 to 6
- key_values: bfloat16 [65536, 1024], P('blk', 'head'), parts along dimension 1, may hold values from -6 to 6
- holding: int32 [128], replicated, may hold values from 0 to 127, as said below
- block_mask: int32 [128, 3], P('blk'), may hold values 0 or 1
Outputs:
- query_grads: bfloat16 [65536, 2048], P('blk', 'head'), parts along dimension 1
- key_value_grads: bfloat16 [65536, 1024], P('blk', 'head'), parts along dimension 1
There are 8 independent parts, one for each index of `head`. A program takes and returns all parts, laid end to end along the dimension named above; an argument that names none is the same for every part. Nothing has to cross between parts.
Inputs may be any that keep to these rules, and one draw needn't show every extreme that they name: `holding`: A permutation of the 128 blocks. Row block t lies on device t // 2; the block it holds belongs (block // 2) to that device or to the one just before or after it. Two neighbouring devices hold the same number of each other's blocks, at most 1; the first two devices and the last two devices always hold exactly 1 of each other's.
All inputs are finite; a program needn't handle non-finite values. No bound on the sum of `block_mask` on one device may be relied on, other than what follows from the above.
Results may differ from a plain program's by a relative error of at most 0.0049.
Values may be sent and summed in bfloat16 or wider, within the bound.
A program may use at most 64 MiB of HBM per device.

v0:
```python
import jax
import jax.numpy as jnp
from jax import lax
from jax.sharding import PartitionSpec as P

HD = 64
QH = 4
BLK_ROWS = 512
BPD = 2


def passed_along(block, axis, distance):
    devices = range(lax.axis_size(axis))
    route = [(i - distance, i) for i in devices if i - distance in devices]
    return lax.ppermute(block, axis, route)


def ranked(offsets, target, slots_out):
    chosen_flags = (offsets == target).astype(jnp.int32)
    rank_order = jnp.cumsum(chosen_flags) - 1
    pick_table = (chosen_flags[None, :] == 1) & (
        rank_order[None, :] == jnp.arange(slots_out)[:, None]
    )
    return pick_table.astype(jnp.float32)


def placing(rank_table, slots, blocks):
    slot_table = (slots[None, :] == jnp.arange(blocks)[:, None]).astype(jnp.float32)
    return jnp.dot(slot_table, rank_table.T, precision=lax.Precision.HIGHEST)


def pick_rows(matrix, stacked):
    return jnp.einsum(
        "cs,jsbk->jcbk", matrix.astype(stacked.dtype), stacked, preferred_element_type=jnp.float32
    )


def pick_stats(matrix, stacked):
    return jnp.einsum("cs,jhsb->jhcb", matrix, stacked, precision=lax.Precision.HIGHEST)


def row_sums(first_rows, second_rows):
    product = first_rows.astype(jnp.float32) * second_rows.astype(jnp.float32)
    return jnp.sum(product.reshape(first_rows.shape[0], QH, HD), axis=2).T


def pair_terms(
    query_block,
    grad_block,
    lse_rows,
    delta_rows,
    key_block,
    first_row,
    first_col,
    alive_flag,
    scaling,
):
    row_count = query_block.shape[0]
    query_heads = query_block.reshape(row_count, QH, HD)
    grad_heads = grad_block.reshape(row_count, QH, HD)
    key_cols = key_block[:, :HD]
    value_cols = key_block[:, HD:]
    scores = (
        jnp.einsum("qhd,kd->hqk", query_heads, key_cols, preferred_element_type=jnp.float32)
        * scaling
    )
    row_ids = first_row + jnp.arange(row_count, dtype=jnp.int32)[:, None]
    col_ids = first_col + jnp.arange(key_block.shape[0], dtype=jnp.int32)[None, :]
    allowed = (col_ids <= row_ids) & (col_ids >= 0) & (alive_flag == 1)
    probs = jnp.where(allowed[None], jnp.exp(scores - lse_rows[:, :, None]), jnp.float32(0.0))
    probs_half = probs.astype(jnp.bfloat16)
    prob_grads = jnp.einsum(
        "qhd,kd->hqk", grad_heads, value_cols, preferred_element_type=jnp.float32
    )
    score_grads = (probs * (prob_grads - delta_rows[:, :, None]) * scaling).astype(jnp.bfloat16)
    query_part = jnp.einsum(
        "hqk,kd->qhd", score_grads, key_cols, preferred_element_type=jnp.float32
    )
    key_part = jnp.einsum(
        "hqk,qhd->kd", score_grads, query_heads, preferred_element_type=jnp.float32
    )
    value_part = jnp.einsum(
        "hqk,qhd->kd", probs_half, grad_heads, preferred_element_type=jnp.float32
    )
    return (query_part.reshape(row_count, QH * HD), jnp.concatenate([key_part, value_part], axis=1))


def on_device(queries, outputs, out_grads, log_sums, key_values, holding, block_mask):
    devices = lax.axis_size("blk")
    device_index = lax.axis_index("blk")
    scaling = HD ** (-0.5)
    spare_slots = BPD // 2
    tok_rows = queries.shape[0]
    prior_values = passed_along(key_values, "blk", 1)

    def owner_map(device_id):
        safe_device = jnp.clip(device_id, 0, devices - 1)
        held_blocks = lax.dynamic_slice_in_dim(holding, safe_device * BPD, BPD)
        return (held_blocks // BPD - device_id, held_blocks % BPD)

    def blocked(array_rows):
        return array_rows.reshape(BPD, BLK_ROWS, array_rows.shape[1])

    stat_shape = (QH, BPD, BLK_ROWS)
    row_stack = jnp.stack([blocked(queries), blocked(outputs), blocked(out_grads)])
    stat_stack = log_sums.reshape((1,) + stat_shape)
    mine_off, mine_slot = owner_map(device_index)
    keep_map = ((mine_off[None, :] == 0) & (mine_slot[None, :] == jnp.arange(BPD)[:, None])).astype(
        jnp.float32
    )
    new_rows = pick_rows(keep_map, row_stack)
    new_stats = pick_stats(keep_map, stat_stack)
    for step_by in (1, -1):
        send_map = ranked(mine_off, step_by, spare_slots)
        got_rows = passed_along(pick_rows(send_map, row_stack).astype(jnp.bfloat16), "blk", step_by)
        got_stats = passed_along(pick_stats(send_map, stat_stack), "blk", step_by)
        source_off, source_slot = owner_map(device_index - step_by)
        placement_map = placing(ranked(source_off, step_by, spare_slots), source_slot, BPD)
        new_rows = new_rows + jnp.einsum(
            "nc,jcbk->jnbk",
            placement_map.astype(jnp.bfloat16),
            got_rows,
            preferred_element_type=jnp.float32,
        )
        new_stats = new_stats + jnp.einsum(
            "nc,jhcb->jhnb", placement_map, got_stats, precision=lax.Precision.HIGHEST
        )
    new_rows = new_rows.astype(jnp.bfloat16)
    query_rows = new_rows[0]
    lse_new = new_stats[0]
    grad_rows = new_rows[2]
    delta_new = row_sums(
        new_rows[1].reshape(tok_rows, QH * HD), grad_rows.reshape(tok_rows, QH * HD)
    ).reshape(stat_shape)
    own_blocks = key_values.reshape(BPD, BLK_ROWS, 2 * HD)
    prior_blocks = prior_values.reshape(BPD, BLK_ROWS, 2 * HD)

    def block_terms(block_idx, lag_blocks, key_blocks, key_idx):
        query_block = lax.dynamic_index_in_dim(query_rows, block_idx, 0, keepdims=False)
        grad_block = lax.dynamic_index_in_dim(grad_rows, block_idx, 0, keepdims=False)
        lse_rows = lax.dynamic_index_in_dim(lse_new, block_idx, 1, keepdims=False)
        delta_rows = lax.dynamic_index_in_dim(delta_new, block_idx, 1, keepdims=False)
        key_block = lax.dynamic_index_in_dim(key_blocks, key_idx, 0, keepdims=False)
        alive_flag = block_mask[block_idx, lag_blocks]
        first_row = (device_index * BPD + block_idx) * BLK_ROWS
        first_col = first_row - lag_blocks * BLK_ROWS
        return pair_terms(
            query_block,
            grad_block,
            lse_rows,
            delta_rows,
            key_block,
            first_row,
            first_col,
            alive_flag,
            scaling,
        )

    query_acc = jnp.zeros((BPD, BLK_ROWS, QH * HD), jnp.float32)
    own_acc = jnp.zeros((BPD, BLK_ROWS, 2 * HD), jnp.float32)
    prior_acc = jnp.zeros((BPD, BLK_ROWS, 2 * HD), jnp.float32)

    def own_outer(block_idx, totals):

        def own_inner(lag_blocks, inner_totals):
            query_sums, key_sums = inner_totals
            query_part, key_part = block_terms(
                block_idx, lag_blocks, own_blocks, block_idx - lag_blocks
            )
            return (
                query_sums.at[block_idx].add(query_part),
                key_sums.at[block_idx - lag_blocks].add(key_part),
            )

        return lax.fori_loop(0, block_idx + 1, own_inner, totals)

    query_acc, own_acc = lax.fori_loop(0, BPD, own_outer, (query_acc, own_acc))

    def prior_outer(block_idx, totals):

        def prior_inner(lag_blocks, inner_totals):
            query_sums, key_sums = inner_totals
            key_idx = block_idx - lag_blocks + BPD
            query_part, key_part = block_terms(block_idx, lag_blocks, prior_blocks, key_idx)
            return (query_sums.at[block_idx].add(query_part), key_sums.at[key_idx].add(key_part))

        return lax.fori_loop(block_idx + 1, BPD + 1, prior_inner, totals)

    query_acc, prior_acc = lax.fori_loop(0, BPD, prior_outer, (query_acc, prior_acc))
    returned = passed_along(prior_acc, "blk", -1)
    key_value_grads = (own_acc + returned).astype(jnp.bfloat16).reshape(tok_rows, 2 * HD)
    query_grads = query_acc.astype(jnp.bfloat16).reshape(tok_rows, QH * HD)
    return (query_grads, key_value_grads)


def solution(mesh):
    in_specs = (
        P("blk", "head"),
        P("blk", "head"),
        P("blk", "head"),
        P("head", "blk"),
        P("blk", "head"),
        P(),
        P("blk", None),
    )
    out_specs = (P("blk", "head"), P("blk", "head"))
    return jax.shard_map(
        on_device, mesh=mesh, in_specs=in_specs, out_specs=out_specs, check_vma=False
    )
```

profile of v0, /device:TPU:254, one launch (start us, length us, event | category | flops | bytes accessed | tf_op | source)
XLA Modules:
  0.0 140.1 jit_solution(12648652832059374419)
XLA Ops:
  0.6 0.8 and_select_fusion.3
  1.5 0.9 compare_convert_fusion.2
  2.5 1.6 %copy_dynamic-update-slice_fusion.2 = bf16[3,2,512,256]{3,1,2,0:T(2,128)(2,1)S(1)} fusion(bf16[1,2,512,256]{3,2,1,0:T(8,128)(2,1)} %bitcast.362), kind=kLoop, calls=%fused_computation.87 | loop fusion | bytes 1048576
  4.1 1.6 %copy_dynamic-update-slice_fusion.1 = bf16[3,2,512,256]{3,1,2,0:T(2,128)(2,1)S(1)} fusion(bf16[3,2,512,256]{3,1,2,0:T(2,128)(2,1)S(1)} %copy_dynamic-update-slice_fusion.2, bf16[1,2,512,256]{3,2,1,0:T(8,128)(2,1)} %bitcast.363), kind=kLoop, calls=%fused_computation.86 | loop fusion | bytes 1048576
  5.7 1.6 %copy_dynamic-update-slice_fusion = bf16[3,2,512,256]{3,1,2,0:T(2,128)(2,1)S(1)} fusion(bf16[3,2,512,256]{3,1,2,0:T(2,128)(2,1)S(1)} %copy_dynamic-update-slice_fusion.1, bf16[1,2,512,256]{3,2,1,0:T(8,128)(2,1)} %bitcast.364), kind=kLoop, calls=%fused_computation.85 | loop fusion | bytes 1048576 | tf_op jit(solution)/shard_map/stack | solution.py:105
  7.3 1.8 %fusion.71 = bf16[1,3,512,256]{3,0,2,1:T(2,128)(2,1)S(1)} fusion(bf16[3,2,512,256]{3,1,2,0:T(2,128)(2,1)S(1)} %copy_dynamic-update-slice_fusion, s32[2,1]{0,1:T(1,128)S(1)} %reduce-window.38, s32[2]{0:T(128)S(1)} %get-tuple-element.1220), kind=kOutput, calls=%fused_computation.147 | convolution fusion | flops 1572880 | bytes 2359312 | tf_op jit(solution)/shard_map/cs,jsbk->jcbk/dot_general | solution.py:33
  9.3 3.3 %collective-permute-start.1 = (bf16[3,1,512,256]{3,2,0,1:T(8,128)(2,1)S(1)}, bf16[3,1,512,256]{3,2,0,1:T(8,128)(2,1)S(1)}, u32[]{:S(2)}, u32[]{:S(2)}) collective-permute-start(bf16[3,1,512,256]{3,2,0,1:T(8,128)(2,1)S(1)} %bitcast.359), channel_id=1, source_target_pairs={{8,0},{16,8},{24,16},{32,24},{40,32},{48,40},{56,48},{64,56},{72,6... | collective-permute-start | bytes 2359304 | tf_op jit(solution)/shard_map/ppermute | solution.py:15
  12.7 1.8 %fusion.70 = bf16[1,3,512,256]{3,0,2,1:T(2,128)(2,1)S(1)} fusion(bf16[3,2,512,256]{3,1,2,0:T(2,128)(2,1)S(1)} %copy_dynamic-update-slice_fusion, s32[2,1]{0,1:T(1,128)S(1)} %reduce-window.36, s32[2]{0:T(128)S(1)} %get-tuple-element.1220), kind=kOutput, calls=%fused_computation.146 | convolution fusion | flops 1572880 | bytes 2359312 | tf_op jit(solution)/shard_map/cs,jsbk->jcbk/dot_general | solution.py:33
  14.7 6.8 %collective-permute-start = (bf16[3,1,512,256]{3,2,0,1:T(8,128)(2,1)S(1)}, bf16[3,1,512,256]{3,2,0,1:T(8,128)(2,1)S(1)}, u32[]{:S(2)}, u32[]{:S(2)}) collective-permute-start(bf16[3,1,512,256]{3,2,0,1:T(8,128)(2,1)S(1)} %bitcast.360), channel_id=1, source_target_pairs={{0,8},{8,16},{16,24},{24,32},{32,40},{40,48},{48,56},{56,64},{64,7... | collective-permute-start | bytes 2359304 | tf_op jit(solution)/shard_map/ppermute | solution.py:15
  21.7 1.9 %collective-permute-start.3 = (f32[1,4,1,512]{3,1,2,0:T(4,128)S(1)}, f32[1,4,1,512]{3,1,2,0:T(4,128)S(1)}, u32[]{:S(2)}, u32[]{:S(2)}) collective-permute-start(f32[1,4,1,512]{3,1,2,0:T(4,128)S(1)} %bitcast.373), channel_id=1, source_target_pairs={{8,0},{16,8},{24,16},{32,24},{40,32},{48,40},{56,48},{64,56},{72,6... | collective-permute-start | bytes 24584 | tf_op jit(solution)/shard_map/ppermute | solution.py:15
  23.8 8.1 %collective-permute-start.2 = (f32[1,4,1,512]{3,1,2,0:T(4,128)S(1)}, f32[1,4,1,512]{3,1,2,0:T(4,128)S(1)}, u32[]{:S(2)}, u32[]{:S(2)}) collective-permute-start(f32[1,4,1,512]{3,1,2,0:T(4,128)S(1)} %bitcast.374), channel_id=1, source_target_pairs={{0,8},{8,16},{16,24},{24,32},{32,40},{40,48},{48,56},{56,64},{64,7... | collective-permute-start | bytes 24584 | tf_op jit(solution)/shard_map/ppermute | solution.py:15
  31.9 1.9 %collective-permute-start.4 = (bf16[1024,128]{1,0:T(8,128)(2,1)}, bf16[1024,128]{1,0:T(8,128)(2,1)}, u32[]{:S(2)}, u32[]{:S(2)}) collective-permute-start(bf16[1024,128]{1,0:T(8,128)(2,1)} %param.27), channel_id=1, source_target_pairs={{0,8},{8,16},{16,24},{24,32},{32,40},{40,48},{48,56},{56,64},{64,7... | collective-permute-start | bytes 786440 | tf_op jit(solution)/shard_map/ppermute | solution.py:15
  33.9 4.8 %fusion.68 = f32[3,512,256,2]{2,3,1,0:T(2,128)} fusion(bf16[3,2,512,256]{3,1,2,0:T(2,128)(2,1)} %copy-done.5, pred[2]{0:T(512)(128)(4,1)S(1)} %get-tuple-element.1225, s32[2]{0:T(128)S(1)} %and_select_fusion.4), kind=kOutput, calls=%fused_computation.145 | convolution fusion | flops 3145744 | bytes 4718602 | tf_op jit(solution)/shard_map/cs,jsbk->jcbk/dot_general | solution.py:33
  39.3 1.1 copy.60
  40.4 12.4 %collective-permute-done.3 = f32[1,4,1,512]{3,1,2,0:T(4,128)S(1)} collective-permute-done((f32[1,4,1,512]{3,1,2,0:T(4,128)S(1)}, f32[1,4,1,512]{3,1,2,0:T(4,128)S(1)}, u32[]{:S(2)}, u32[]{:S(2)}) %collective-permute-start.3) | collective-permute-done | bytes 8224 | tf_op jit(solution)/shard_map/ppermute | solution.py:15
  53.6 1.8 %copy.65 = bf16[2,512,128]{1,2,0:T(8,128)(2,1)} copy(bf16[2,512,128]{2,1,0:T(8,128)(2,1)} %bitcast.83) | data formatting | bytes 524288 | tf_op jit(solution)/shard_map/while | solution.py:189
  55.7 1.6 %copy-done.2 = f32[3,512,256,2]{2,3,1,0:T(2,128)S(1)} copy-done((f32[3,512,256,2]{2,3,1,0:T(2,128)S(1)}, f32[3,512,256,2]{2,3,1,0:T(2,128)}, u32[]{:S(2)}) %copy-start.2) | copy-done | bytes 3145752
  58.1 0.9 slice_bitcast_fusion.11
  59.6 0.9 mul.111
  60.5 1.3 copy.56
  61.7 1.0 copy.58
  63.0 27.9 %while.102 = (s32[]{:T(128)}, f32[2,512,256]{1,2,0:T(8,128)S(1)}, f32[2,512,128]{1,2,0:T(8,128)S(1)}, s32[]{:T(128)}, bf16[2,512,256]{1,2,0:T(8,128)(2,1)S(1)}, ...) while((s32[]{:T(128)}, f32[2,512,256]{1,2,0:T(8,128)S(1)}, ...), condition=%wide.region_10.11_spmd, body=%wide.region_5.10_spmd.sunk | while | flops 683870208 | bytes 25429856 | solution.py:177
  63.1 1.0 constant_dynamic-slice_fusion.12
  64.2 8.6 %while.105 = (s32[]{:T(128)}, f32[2,512,256]{1,2,0:T(8,128)S(1)}, f32[2,512,128]{1,2,0:T(8,128)S(1)}, s32[]{:T(128)}, s32[3]{0:T(128)S(1)}, /*index=5*/pred[3]{0...) while((s32[]{:T(128)}, f32[2,512,256]{1,2,0:T(8,128)S(1)}, ...), condition=%wide.region_9.9_spmd, body=%wide.region_6.8_spmd.sunk | while | flops 683870208 | bytes 24348032 | solution.py:175
  66.6 1.7 %fusion.158 = bf16[4,512,512]{1,2,0:T(8,128)(2,1)S(1)} fusion(f32[512,512,4]{1,0,2:T(8,128)S(1)} %fusion.157, bf16[512,4,64]{0,2,1:T(8,128)(2,1)S(1)} %bitcast.357, f32[4,512]{1,0:T(4,128)S(1)} %bitcast.370, f32[4,512]{1,0:T(4,128)S(1)} %bitcast.371, pred[512,512]{0,1:T(8,128)(4,1)S(1)} %and_and_fusion.5, ...), kind=kOutput, calls=%fused_computation.3.clone.1 | convolution fusion | flops 141557760 | bytes 6897664 | tf_op jit(solution)/shard_map/while/body/eval_jaxpr/while/body/qhd,kd->hqk/dot_general | solution.py:72
  68.3 0.7 convolution_bitcast_fusion.8
  69.0 1.0 fusion.161
  70.0 0.8 and_reduce_fusion.7
  72.0 0.8 fusion.160
  72.8 1.0 constant_dynamic-slice_fusion.12
  73.9 17.1 %while.105 = (s32[]{:T(128)}, f32[2,512,256]{1,2,0:T(8,128)S(1)}, f32[2,512,128]{1,2,0:T(8,128)S(1)}, s32[]{:T(128)}, s32[3]{0:T(128)S(1)}, /*index=5*/pred[3]{0...) while((s32[]{:T(128)}, f32[2,512,256]{1,2,0:T(8,128)S(1)}, ...), condition=%wide.region_9.9_spmd, body=%wide.region_6.8_spmd.sunk | while | flops 683870208 | bytes 24348032 | solution.py:175
  76.3 1.7 %fusion.158 = bf16[4,512,512]{1,2,0:T(8,128)(2,1)S(1)} fusion(f32[512,512,4]{1,0,2:T(8,128)S(1)} %fusion.157, bf16[512,4,64]{0,2,1:T(8,128)(2,1)S(1)} %bitcast.357, f32[4,512]{1,0:T(4,128)S(1)} %bitcast.370, f32[4,512]{1,0:T(4,128)S(1)} %bitcast.371, pred[512,512]{0,1:T(8,128)(4,1)S(1)} %and_and_fusion.5, ...), kind=kOutput, calls=%fused_computation.3.clone.1 | convolution fusion | flops 141557760 | bytes 6897664 | tf_op jit(solution)/shard_map/while/body/eval_jaxpr/while/body/qhd,kd->hqk/dot_general | solution.py:72
  77.9 0.7 convolution_bitcast_fusion.8
  78.7 1.0 fusion.161
  79.7 0.8 and_reduce_fusion.7
  81.6 0.8 fusion.160
  84.8 1.7 %fusion.158 = bf16[4,512,512]{1,2,0:T(8,128)(2,1)S(1)} fusion(f32[512,512,4]{1,0,2:T(8,128)S(1)} %fusion.157, bf16[512,4,64]{0,2,1:T(8,128)(2,1)S(1)} %bitcast.357, f32[4,512]{1,0:T(4,128)S(1)} %bitcast.370, f32[4,512]{1,0:T(4,128)S(1)} %bitcast.371, pred[512,512]{0,1:T(8,128)(4,1)S(1)} %and_and_fusion.5, ...), kind=kOutput, calls=%fused_computation.3.clone.1 | convolution fusion | flops 141557760 | bytes 6897664 | tf_op jit(solution)/shard_map/while/body/eval_jaxpr/while/body/qhd,kd->hqk/dot_general | solution.py:72
  86.5 0.7 convolution_bitcast_fusion.8
  87.3 1.0 fusion.161
  88.3 0.8 and_reduce_fusion.7
  90.2 0.8 fusion.160
  91.8 27.5 %while.104 = (s32[]{:T(128)}, f32[2,512,256]{1,2,0:T(8,128)S(1)}, f32[2,512,128]{1,2,0:T(8,128)S(1)}, s32[]{:T(128)}, bf16[2,512,256]{1,2,0:T(8,128)(2,1)S(1)}, ...) while((s32[]{:T(128)}, f32[2,512,256]{1,2,0:T(8,128)S(1)}, ...), condition=%wide.region_16.17_spmd, body=%wide.region_11.16_spmd.sunk | while | flops 683870208 | bytes 25429860 | solution.py:189
  91.8 1.0 constant_dynamic-slice_fusion.14
  92.9 16.9 %while.106 = (s32[]{:T(128)}, f32[2,512,256]{1,2,0:T(8,128)S(1)}, f32[2,512,128]{1,2,0:T(8,128)S(1)}, s32[3]{0:T(128)S(1)}, pred[3]{0:T(512)(128)(4,1)S(1)}, /*i...) while((s32[]{:T(128)}, f32[2,512,256]{1,2,0:T(8,128)S(1)}, ...), condition=%wide.region_15.15_spmd, body=%wide.region_12.14_spmd.sunk | while | flops 683870208 | bytes 24348044 | solution.py:187
  95.2 1.7 %fusion.145 = bf16[4,512,512]{1,2,0:T(8,128)(2,1)S(1)} fusion(f32[512,512,4]{1,0,2:T(8,128)S(1)} %fusion.144, bf16[512,4,64]{0,2,1:T(8,128)(2,1)S(1)} %bitcast.355, f32[4,512]{1,0:T(4,128)S(1)} %bitcast.367, f32[4,512]{1,0:T(4,128)S(1)} %bitcast.368, pred[512,512]{0,1:T(8,128)(4,1)S(1)} %and_and_fusion.4, ...), kind=kOutput, calls=%fused_computation.38.clone.1 | convolution fusion | flops 141557760 | bytes 6897664 | tf_op jit(solution)/shard_map/while/body/eval_jaxpr/while/body/qhd,kd->hqk/dot_general | solution.py:72
  96.8 0.7 convolution_bitcast_fusion.7
  97.6 1.0 fusion.148
  98.6 0.8 and_reduce_fusion.6
  100.5 0.8 fusion.147
  103.6 1.7 %fusion.145 = bf16[4,512,512]{1,2,0:T(8,128)(2,1)S(1)} fusion(f32[512,512,4]{1,0,2:T(8,128)S(1)} %fusion.144, bf16[512,4,64]{0,2,1:T(8,128)(2,1)S(1)} %bitcast.355, f32[4,512]{1,0:T(4,128)S(1)} %bitcast.367, f32[4,512]{1,0:T(4,128)S(1)} %bitcast.368, pred[512,512]{0,1:T(8,128)(4,1)S(1)} %and_and_fusion.4, ...), kind=kOutput, calls=%fused_computation.38.clone.1 | convolution fusion | flops 141557760 | bytes 6897664 | tf_op jit(solution)/shard_map/while/body/eval_jaxpr/while/body/qhd,kd->hqk/dot_general | solution.py:72
  106.0 1.0 fusion.148
  107.0 0.8 and_reduce_fusion.6
  109.0 0.8 fusion.147
  109.8 1.0 constant_dynamic-slice_fusion.14
  110.8 8.4 %while.106 = (s32[]{:T(128)}, f32[2,512,256]{1,2,0:T(8,128)S(1)}, f32[2,512,128]{1,2,0:T(8,128)S(1)}, s32[3]{0:T(128)S(1)}, pred[3]{0:T(512)(128)(4,1)S(1)}, /*i...) while((s32[]{:T(128)}, f32[2,512,256]{1,2,0:T(8,128)S(1)}, ...), condition=%wide.region_15.15_spmd, body=%wide.region_12.14_spmd.sunk | while | flops 683870208 | bytes 24348044 | solution.py:187
  113.2 1.7 %fusion.145 = bf16[4,512,512]{1,2,0:T(8,128)(2,1)S(1)} fusion(f32[512,512,4]{1,0,2:T(8,128)S(1)} %fusion.144, bf16[512,4,64]{0,2,1:T(8,128)(2,1)S(1)} %bitcast.355, f32[4,512]{1,0:T(4,128)S(1)} %bitcast.367, f32[4,512]{1,0:T(4,128)S(1)} %bitcast.368, pred[512,512]{0,1:T(8,128)(4,1)S(1)} %and_and_fusion.4, ...), kind=kOutput, calls=%fused_computation.38.clone.1 | convolution fusion | flops 141557760 | bytes 6897664 | tf_op jit(solution)/shard_map/while/body/eval_jaxpr/while/body/qhd,kd->hqk/dot_general | solution.py:72
  115.6 1.0 fusion.148
  116.6 0.8 and_reduce_fusion.6
  118.5 0.8 fusion.147
  119.3 3.3 %collective-permute-start.5 = (f32[2,512,128]{1,2,0:T(8,128)S(1)}, f32[2,512,128]{1,2,0:T(8,128)S(1)}, u32[]{:S(2)}, u32[]{:S(2)}) collective-permute-start(f32[2,512,128]{1,2,0:T(8,128)S(1)} %get-tuple-element.1893), channel_id=1, source_target_pairs={{8,0},{16,8},{24,16},{32,24},{40,32},{48,40},{56,48},{64,56},{72,6... | collective-permute-start | bytes 1572872 | tf_op jit(solution)/shard_map/ppermute | solution.py:15
  122.6 1.0 copy.66
  123.6 14.6 %collective-permute-done.5 = f32[2,512,128]{1,2,0:T(8,128)S(1)} collective-permute-done((f32[2,512,128]{1,2,0:T(8,128)S(1)}, f32[2,512,128]{1,2,0:T(8,128)S(1)}, u32[]{:S(2)}, u32[]{:S(2)}) %collective-permute-start.5) | collective-permute-done | bytes 524320 | tf_op jit(solution)/shard_map/ppermute | solution.py:15
  138.2 1.1 add_convert_fusion
  139.3 0.8 copy.67
  (102 shorter events, 23.8 us)
Async XLA Ops:
  7.3 5.4 %copy-start.5 = (bf16[3,2,512,256]{3,1,2,0:T(2,128)(2,1)}, bf16[3,2,512,256]{3,1,2,0:T(2,128)(2,1)S(1)}, u32[]{:S(2)}) copy-start(bf16[3,2,512,256]{3,1,2,0:T(2,128)(2,1)S(1)} %copy_dynamic-update-slice_fusion) | copy-start | bytes 4718596
  9.3 46.2 %collective-permute-start.1 = (bf16[3,1,512,256]{3,2,0,1:T(8,128)(2,1)S(1)}, bf16[3,1,512,256]{3,2,0,1:T(8,128)(2,1)S(1)}, u32[]{:S(2)}, u32[]{:S(2)}) collective-permute-start(bf16[3,1,512,256]{3,2,0,1:T(8,128)(2,1)S(1)} %bitcast.359), channel_id=1, source_target_pairs={{8,0},{16,8},{24,16},{32,24},{40,32},{48,40},{56,48},{64,56},{72,6... | collective-permute-start | bytes 2359304 | tf_op jit(solution)/shard_map/ppermute | solution.py:15
  12.7 8.8 %copy-start.6 = (f32[4,1024]{1,0:T(4,128)S(1)}, f32[4,1024]{1,0:T(4,128)}, u32[]{:S(2)}) copy-start(f32[4,1024]{1,0:T(4,128)} %param.26) | copy-start | bytes 49156
  14.7 40.9 %collective-permute-start = (bf16[3,1,512,256]{3,2,0,1:T(8,128)(2,1)S(1)}, bf16[3,1,512,256]{3,2,0,1:T(8,128)(2,1)S(1)}, u32[]{:S(2)}, u32[]{:S(2)}) collective-permute-start(bf16[3,1,512,256]{3,2,0,1:T(8,128)(2,1)S(1)} %bitcast.360), channel_id=1, source_target_pairs={{0,8},{8,16},{16,24},{24,32},{32,40},{40,48},{48,56},{56,64},{64,7... | collective-permute-start | bytes 2359304 | tf_op jit(solution)/shard_map/ppermute | solution.py:15
  21.7 31.2 %collective-permute-start.3 = (f32[1,4,1,512]{3,1,2,0:T(4,128)S(1)}, f32[1,4,1,512]{3,1,2,0:T(4,128)S(1)}, u32[]{:S(2)}, u32[]{:S(2)}) collective-permute-start(f32[1,4,1,512]{3,1,2,0:T(4,128)S(1)} %bitcast.373), channel_id=1, source_target_pairs={{8,0},{16,8},{24,16},{32,24},{40,32},{48,40},{56,48},{64,56},{72,6... | collective-permute-start | bytes 24584 | tf_op jit(solution)/shard_map/ppermute | solution.py:15
  23.8 29.1 %collective-permute-start.2 = (f32[1,4,1,512]{3,1,2,0:T(4,128)S(1)}, f32[1,4,1,512]{3,1,2,0:T(4,128)S(1)}, u32[]{:S(2)}, u32[]{:S(2)}) collective-permute-start(f32[1,4,1,512]{3,1,2,0:T(4,128)S(1)} %bitcast.374), channel_id=1, source_target_pairs={{0,8},{8,16},{16,24},{24,32},{32,40},{40,48},{48,56},{56,64},{64,7... | collective-permute-start | bytes 24584 | tf_op jit(solution)/shard_map/ppermute | solution.py:15
  31.9 21.7 %collective-permute-start.4 = (bf16[1024,128]{1,0:T(8,128)(2,1)}, bf16[1024,128]{1,0:T(8,128)(2,1)}, u32[]{:S(2)}, u32[]{:S(2)}) collective-permute-start(bf16[1024,128]{1,0:T(8,128)(2,1)} %param.27), channel_id=1, source_target_pairs={{0,8},{8,16},{16,24},{24,32},{32,40},{40,48},{48,56},{56,64},{64,7... | collective-permute-start | bytes 786440 | tf_op jit(solution)/shard_map/ppermute | solution.py:15
  55.4 1.9 %copy-start.2 = (f32[3,512,256,2]{2,3,1,0:T(2,128)S(1)}, f32[3,512,256,2]{2,3,1,0:T(2,128)}, u32[]{:S(2)}) copy-start(f32[3,512,256,2]{2,3,1,0:T(2,128)} %fusion.68) | copy-start | bytes 9437188
  59.5 3.5 %copy-start.3 = (s32[3]{0:T(128)S(1)}, s32[3]{0:T(128)}, u32[]{:S(2)}) copy-start(s32[3]{0:T(128)} %constant.368.clone.1) | copy-start | bytes 40
  59.6 3.5 %copy-start.4 = (s32[2,3]{1,0:T(2,128)S(1)}, s32[2,3]{1,0:T(2,128)}, u32[]{:S(2)}) copy-start(s32[2,3]{1,0:T(2,128)} %param.29) | copy-start | bytes 76
  63.0 28.0 %copy-start.1 = (bf16[2,512,128]{1,2,0:T(8,128)(2,1)S(1)}, bf16[2,512,128]{1,2,0:T(8,128)(2,1)}, u32[]{:S(2)}) copy-start(bf16[2,512,128]{1,2,0:T(8,128)(2,1)} %copy.65) | copy-start | bytes 786436
  91.0 0.8 copy-start
  119.3 18.9 %collective-permute-start.5 = (f32[2,512,128]{1,2,0:T(8,128)S(1)}, f32[2,512,128]{1,2,0:T(8,128)S(1)}, u32[]{:S(2)}, u32[]{:S(2)}) collective-permute-start(f32[2,512,128]{1,2,0:T(8,128)S(1)} %get-tuple-element.1893), channel_id=1, source_target_pairs={{8,0},{16,8},{24,16},{32,24},{40,32},{48,40},{56,48},{64,56},{72,6... | collective-permute-start | bytes 1572872 | tf_op jit(solution)/shard_map/ppermute | solution.py:15
where the time goes:
time: 141 us; the launch traced here: 140 us
  matrix products  36.8 us (26%)
  waiting for transfers between devices  27.6 us (20%)
  starting transfers between devices  25.3 us (18%)
  local copies, waits for them, and re-layouts  24.9 us (18%)
  other arithmetic  19.9 us (14%)
  loops' own time  4.6 us (3%)
    ppermute x6, waiting for transfers between devices, passed_along(): return lax.ppermute(block, axis, route)  27.6 us
    ppermute x6, starting transfers between devices, passed_along(): return lax.ppermute(block, axis, route)  25.3 us
    dot_general x6, matrix products, pair_terms(): jnp.einsum('qhd,kd->hqk', grad_heads, value_cols, preferred_element_type=...  9.95 us
    dot_general x3, matrix products, pick_rows(): jnp.einsum('cs,jsbk->jcbk', matrix.astype(stacked.dtype), stacked, prefer...  8.38 us
    dot_general x6, matrix products, pair_terms(): jnp.einsum('hqk,qhd->kd', probs_half, grad_heads, preferred_element_type=...  6.07 us
    another operation x17, other arithmetic  5.89 us
    unnamed x16, local copies, waits for them, and re-layouts  5.54 us
    dot_general x6, matrix products, pair_terms(): jnp.einsum('hqk,qhd->kd', score_grads, query_heads, preferred_element_typ...  4.46 us
  transfers between devices with their start and end apart: 6, of which 3 were waited for; matrix products, arithmetic and copies ran while one was open for 9% of the time, Pallas kernels for 0%

commit v1 on v0

v1 whole, which is shorter than its diff:
```python
import functools

import jax
import jax.numpy as jnp
from jax import lax
from jax.experimental import pallas as pl
from jax.experimental.pallas import tpu as pltpu
from jax.sharding import PartitionSpec as P

HD = 64
QH = 4
BLK = 512
BPD = 2
SPAN = 3
ROWS = BPD * BLK
HALF = 256
NCH = 4
LOG2E = 1.4426950408889634
SCALE = HD**-0.5
DEAD = 1e30
MESH = pl.DeviceIdType.MESH
F32 = jnp.float32
BF16 = jnp.bfloat16


def nt(a, b):
    return lax.dot_general(a, b, (((1,), (1,)), ((), ())), preferred_element_type=F32)


def nn(a, b):
    return lax.dot_general(a, b, (((1,), (0,)), ((), ())), preferred_element_type=F32)


def pick(cond, a, b):
    return lax.select(jnp.broadcast_to(cond, a.shape), a, b)


def kernel(
    n,
    q_ref, o_ref, do_ref, lse_ref, kv_ref, holding_ref, mask_ref,
    dq_ref, dkv_ref,
    qv, ov, dov, lsev, kvw, ktw, sendb, recvb, stat_send, stat_pool, lsew, deltaw, wbuf,
    acc, dqt, dqo, dkv_send, dkv_in, dkv_out,
    load_sem, out_sem, send_sem, recv_sem,
):
    me = lax.axis_index("blk")
    nxt = lax.rem(me + 1, n)
    prv = lax.rem(me + n - 1, n)

    loads = []
    for p in range(2):
        cols = pl.ds(p * 128, 128)
        loads.append(pltpu.make_async_copy(q_ref.at[:, cols], qv.at[p], load_sem.at[3 * p]))
        loads.append(pltpu.make_async_copy(do_ref.at[:, cols], dov.at[p], load_sem.at[3 * p + 1]))
        loads.append(pltpu.make_async_copy(o_ref.at[:, cols], ov.at[p], load_sem.at[3 * p + 2]))
    load_lse = pltpu.make_async_copy(lse_ref, lsev, load_sem.at[6])
    load_kv = pltpu.make_async_copy(kv_ref, kvw.at[pl.ds(ROWS, ROWS)], load_sem.at[7])
    load_kv.start()
    for c in loads:
        c.start()
    load_lse.start()

    barrier = pltpu.get_barrier_semaphore()
    for dev in (prv, nxt):
        pl.semaphore_signal(barrier, inc=1, device_id={"blk": dev}, device_id_type=MESH)
    pl.semaphore_wait(barrier, 2)

    def remote(src, dst, idx, dev):
        return pltpu.make_async_remote_copy(
            src_ref=src, dst_ref=dst, send_sem=send_sem.at[idx], recv_sem=recv_sem.at[idx],
            device_id={"blk": dev}, device_id_type=MESH,
        )

    kv_copy = remote(kvw.at[pl.ds(ROWS, ROWS)], kvw.at[pl.ds(0, ROWS)], 0, nxt)
    stat_copies = [
        remote(stat_send.at[0], stat_pool.at[2], 1, nxt),
        remote(stat_send.at[1], stat_pool.at[3], 2, prv),
    ]

    def row_copy(j, side):
        return remote(sendb.at[side, j], recvb.at[side, j], 4 + 2 * j + side, nxt if side == 0 else prv)

    dkv_copy = remote(dkv_send, dkv_in, 3, prv)

    load_kv.wait()
    kv_copy.start()

    h0 = holding_ref[2 * me]
    h1 = holding_ref[2 * me + 1]
    p0 = holding_ref[2 * prv]
    p1 = holding_ref[2 * prv + 1]
    second = [(h1 >> 1) == me + 1, (h1 >> 1) == me - 1]
    for c in loads:
        c.wait()
    for j in range(NCH):
        t, p = j // 2, j % 2
        first_rows = pl.ds(t * HALF, HALF)
        second_rows = pl.ds(BLK + t * HALF, HALF)
        for side in range(2):
            for a, src in enumerate((qv, dov)):
                sendb[side, j, a] = pick(second[side], src[p, second_rows, :], src[p, first_rows, :])
            row_copy(j, side).start()

    load_lse.wait()
    head_of = lax.broadcasted_iota(jnp.int32, (8, 128), 1) // HD
    row_of = lax.broadcasted_iota(jnp.int32, (8, 128), 0)
    delta = jnp.zeros((8, ROWS), F32)
    for p in range(2):
        prod = ov[p].astype(F32) * dov[p].astype(F32)
        hi = prod.astype(BF16)
        lo = (prod - hi.astype(F32)).astype(BF16)
        ind = (row_of == head_of + 4 + 2 * p).astype(BF16)
        delta = delta + nt(ind, hi) + nt(ind, lo)
    for slot in range(BPD):
        cols = pl.ds(slot * BLK, BLK)
        stat_pool[slot, 4:8, :] = delta[4:8, slot * BLK : (slot + 1) * BLK]
        stat_pool[slot, 0:4, :] = lsev[:, cols] * LOG2E
    for side in range(2):
        stat_send[side] = pick(second[side], stat_pool[1], stat_pool[0])
        stat_copies[side].start()

    def transpose_keys(base):
        for i in range(ROWS // HALF):
            kt = kvw[pl.ds(base + i * HALF, HALF), :].astype(F32).T
            ktw[base // HALF + i] = kt[:HD].astype(BF16)

    transpose_keys(ROWS)
    acc[...] = jnp.zeros_like(acc)

    for c in stat_copies:
        c.wait_recv()
    is0, is1, isp = [], [], []
    for s in range(BPD):
        b = BPD * me + s
        is0.append(h0 == b)
        is1.append(h1 == b)
        isp.append((p0 == b) | (p1 == b))

    def choose(s, own0, own1, before, after):
        return pick(is0[s], own0, pick(is1[s], own1, pick(isp[s], before, after)))

    for s in range(BPD):
        st = choose(s, stat_pool[0], stat_pool[1], stat_pool[2], stat_pool[3])
        for w in range(SPAN):
            alive = (mask_ref[s, w] == 1) & (BPD * me + s >= w)
            bias = jnp.where(alive, 0.0, DEAD).astype(F32)
            lw = st + bias
            for h in range(QH):
                for t in range(2):
                    lsew[s, w, t, h] = lw[h : h + 1, t * HALF : (t + 1) * HALF]
        for h in range(QH):
            for t in range(2):
                deltaw[s, t, h] = st[4 + h : 5 + h, t * HALF : (t + 1) * HALF]

    kv_copy.wait_recv()
    transpose_keys(0)

    low = lax.broadcasted_iota(jnp.int32, (HALF, 128), 1) < HD
    causal = lax.broadcasted_iota(jnp.int32, (HALF, HALF), 0) <= lax.broadcasted_iota(
        jnp.int32, (HALF, HALF), 1
    )

    def unit(j, s, ct, masked):
        t, p = j // 2, j % 2
        tile = 2 * s + ct
        rows = pl.ds(pl.multiple_of(tile * HALF, HALF), HALF)
        kv = kvw[rows, :]
        kt = ktw[tile]
        w = 2 - ct // 2
        total = acc[rows, :]
        for hp in range(2):
            w1 = wbuf[s, hp, 0]
            w2 = wbuf[s, hp, 1]
            h = 2 * p + hp
            x = nt(kv, w1) * (SCALE * LOG2E) - lsew[s, w, t, h]
            probs = jnp.exp2(x)
            if masked:
                probs = jnp.where(causal, probs, 0.0)
            ds = (probs * (nt(kv, w2) - deltaw[s, t, h])).astype(BF16)
            total = total + nn(ds, w1) + nn(probs.astype(BF16), w2)
            dqt[s, pl.ds(hp * HD, HD), :] += nn(kt, ds)
        acc[rows, :] = total

    def chunk(j, _):
        t, p = j // 2, j % 2
        row_copy(j, 0).wait_recv()
        row_copy(j, 1).wait_recv()
        for s in range(BPD):
            rows0 = pl.ds(pl.multiple_of(t * HALF, HALF), HALF)
            rows1 = pl.ds(pl.multiple_of(BLK + t * HALF, HALF), HALF)
            qs = choose(s, qv[p, rows0, :], qv[p, rows1, :], recvb[0, j, 0], recvb[1, j, 0]).astype(F32)
            ds = choose(s, dov[p, rows0, :], dov[p, rows1, :], recvb[0, j, 1], recvb[1, j, 1]).astype(F32)
            wbuf[s, 0, 0] = jnp.where(low, qs, 0.0).astype(BF16)
            wbuf[s, 1, 0] = jnp.where(low, pltpu.roll(qs, HD, 1), 0.0).astype(BF16)
            wbuf[s, 0, 1] = jnp.where(low, 0.0, pltpu.roll(ds, HD, 1)).astype(BF16)
            wbuf[s, 1, 1] = jnp.where(low, 0.0, ds).astype(BF16)
        dqt[...] = jnp.zeros_like(dqt)

        def run(s, lo, hi):
            lax.fori_loop(lo, hi, lambda ct, _: (unit(j, s, ct, False), 0)[1], 0)

        run(0, 0, 4)
        run(1, 0, 2)

        @pl.when(j == NCH - 1)
        def _():
            scaled = jnp.where(low[:1], SCALE, 1.0)
            for i in range(ROWS // HALF):
                r = pl.ds(i * HALF, HALF)
                dkv_send[r, :] = (acc[r, :] * scaled).astype(BF16)
            dkv_copy.start()

        run(0, 4, 4 + t)
        unit(j, 0, 4 + t, True)
        run(1, 2, 4 + t)
        unit(j, 1, 4 + t, True)
        for s in range(BPD):
            dqo[j, s] = (dqt[s].T * SCALE).astype(BF16)
        return 0

    lax.fori_loop(0, NCH, chunk, 0)

    dq_copies = []
    for j in range(NCH):
        t, p = j // 2, j % 2
        for s in range(BPD):
            dst = dq_ref.at[pl.ds(s * BLK + t * HALF, HALF), pl.ds(p * 128, 128)]
            c = pltpu.make_async_copy(dqo.at[j, s], dst, out_sem.at[2 * j + s])
            c.start()
            dq_copies.append(c)

    dkv_copy.wait_recv()
    scaled = jnp.where(low[:1], SCALE, 1.0)
    for i in range(ROWS // HALF):
        r = pl.ds(i * HALF, HALF)
        own = acc[pl.ds(ROWS + i * HALF, HALF), :] * scaled
        dkv_out[r, :] = (own + dkv_in[r, :].astype(F32)).astype(BF16)
    dkv_store = pltpu.make_async_copy(dkv_out, dkv_ref, out_sem.at[8])
    dkv_store.start()

    kv_copy.wait_send()
    for c in stat_copies:
        c.wait_send()
    for j in range(NCH):
        for side in range(2):
            row_copy(j, side).wait_send()
    dkv_copy.wait_send()
    for c in dq_copies:
        c.wait()
    dkv_store.wait()


def on_device(n, queries, outputs, out_grads, log_sums, key_values, holding, block_mask):
    hbm = pl.BlockSpec(memory_space=pl.ANY)
    smem = pl.BlockSpec(memory_space=pltpu.SMEM)
    vm = pltpu.VMEM
    return pl.pallas_call(
        functools.partial(kernel, n),
        out_shape=(
            jax.ShapeDtypeStruct((ROWS, QH * HD), BF16),
            jax.ShapeDtypeStruct((ROWS, 2 * HD), BF16),
        ),
        in_specs=[hbm] * 5 + [smem] * 2,
        out_specs=(hbm, hbm),
        scratch_shapes=[
            vm((2, ROWS, 128), BF16),
            vm((2, ROWS, 128), BF16),
            vm((2, ROWS, 128), BF16),
            vm((QH, ROWS), F32),
            vm((2 * ROWS, 128), BF16),
            vm((2 * ROWS // HALF, HD, HALF), BF16),
            vm((2, NCH, 2, HALF, 128), BF16),
            vm((2, NCH, 2, HALF, 128), BF16),
            vm((2, 8, BLK), F32),
            vm((4, 8, BLK), F32),
            vm((BPD, SPAN, 2, QH, 1, HALF), F32),
            vm((BPD, 2, QH, 1, HALF), F32),
            vm((BPD, 2, 2, HALF, 128), BF16),
            vm((2 * ROWS, 128), F32),
            vm((BPD, 128, HALF), F32),
            vm((NCH, BPD, HALF, 128), BF16),
            vm((ROWS, 128), BF16),
            vm((ROWS, 128), BF16),
            vm((ROWS, 128), BF16),
            pltpu.SemaphoreType.DMA((8,)),
            pltpu.SemaphoreType.DMA((9,)),
            pltpu.SemaphoreType.DMA((12,)),
            pltpu.SemaphoreType.DMA((12,)),
        ],
        compiler_params=pltpu.CompilerParams(
            collective_id=0, has_side_effects=True, vmem_limit_bytes=40 * 1024 * 1024
        ),
    )(queries, outputs, out_grads, log_sums, key_values, holding, block_mask)


def solution(mesh):
    in_specs = (
        P("blk", "head"),
        P("blk", "head"),
        P("blk", "head"),
        P("head", "blk"),
        P("blk", "head"),
        P(),
        P("blk", None),
    )
    out_specs = (P("blk", "head"), P("blk", "head"))
    return jax.shard_map(
        functools.partial(on_device, mesh.shape["blk"]),
        mesh=mesh, in_specs=in_specs, out_specs=out_specs, check_vma=False,
    )
```

time: 141 us -> 84.2 us (0.60)
  the two profiles are of different devices: /device:TPU:254 before, /device:TPU:16 now
where the time goes in v1:
time: 84.2 us; the launch traced here: 83.8 us
  Pallas kernels  75.6 us (90%)
  local copies, waits for them, and re-layouts  7.61 us (9%)
    pallas_call x1, Pallas kernels, on_device(): pl.pallas_call(functools.partial(kernel, n), out_shape=(jax.ShapeDtypeStr...  75.6 us
    unnamed x16, local copies, waits for them, and re-layouts  7.61 us

profile of v1, /device:TPU:16, one launch (start us, length us, event | category | flops | bytes accessed | tf_op | source)
XLA Modules:
  0.0 83.8 jit_solution(6001646172030734350)
XLA Ops:
  0.6 0.0 copy-start
  0.6 1.0 %copy-done = bf16[1024,256]{1,0:T(8,128)(2,1)S(1)} copy-done((bf16[1024,256]{1,0:T(8,128)(2,1)S(1)}, bf16[1024,256]{1,0:T(8,128)(2,1)}, u32[]{:S(2)}) %copy-start) | copy-done | bytes 524312
  1.7 0.0 copy-start.1
  1.7 1.0 %copy-done.1 = bf16[1024,256]{1,0:T(8,128)(2,1)S(1)} copy-done((bf16[1024,256]{1,0:T(8,128)(2,1)S(1)}, bf16[1024,256]{1,0:T(8,128)(2,1)}, u32[]{:S(2)}) %copy-start.1) | copy-done | bytes 524312
  2.7 0.0 copy-start.2
  2.7 1.0 %copy-done.2 = bf16[1024,256]{1,0:T(8,128)(2,1)S(1)} copy-done((bf16[1024,256]{1,0:T(8,128)(2,1)S(1)}, bf16[1024,256]{1,0:T(8,128)(2,1)}, u32[]{:S(2)}) %copy-start.2) | copy-done | bytes 524312
  3.8 0.0 copy-start.3
  3.8 0.9 %copy-done.3 = bf16[1024,128]{1,0:T(8,128)(2,1)S(1)} copy-done((bf16[1024,128]{1,0:T(8,128)(2,1)S(1)}, bf16[1024,128]{1,0:T(8,128)(2,1)}, u32[]{:S(2)}) %copy-start.3) | copy-done | bytes 262168
  4.7 0.0 copy-start.4
  4.7 0.7 copy-done.4
  5.4 0.0 copy-start.5
  5.4 0.7 copy-done.5
  6.1 0.0 copy-start.6
  6.1 0.7 copy-done.6
  6.8 75.6 %shard_map.86 = (bf16[1024,256]{1,0:T(8,128)(2,1)S(1)}, bf16[1024,128]{1,0:T(8,128)(2,1)S(1)}) custom-call(bf16[1024,256]{1,0:T(8,128)(2,1)S(1)} %copy-done, bf16[1024,256]{1,0:T(8,128)(2,1)S(1)} %copy-done.1, bf16[1024,256]{1,0:T(8,128)(2,1)S(1)} %copy-done.2, f32[4,1024]{1,0:T(4,128)S(1)} %copy-done.4, bf16[1024,128]{1,0:T(8,128)(2,1)S(1)} %copy-done.3, ...), custom_call_target="tpu_custom_call" | custom-call | tf_op jit(solution)/shard_map/pallas_call | solution.py:257
  82.3 0.8 copy.11
  83.1 0.7 copy.12
Async XLA Ops:
  0.6 1.0 %copy-start = (bf16[1024,256]{1,0:T(8,128)(2,1)S(1)}, bf16[1024,256]{1,0:T(8,128)(2,1)}, u32[]{:S(2)}) copy-start(bf16[1024,256]{1,0:T(8,128)(2,1)} %q_ref.1) | copy-start | bytes 1572868
  1.7 1.0 %copy-start.1 = (bf16[1024,256]{1,0:T(8,128)(2,1)S(1)}, bf16[1024,256]{1,0:T(8,128)(2,1)}, u32[]{:S(2)}) copy-start(bf16[1024,256]{1,0:T(8,128)(2,1)} %o_ref.1) | copy-start | bytes 1572868
  2.7 1.0 %copy-start.2 = (bf16[1024,256]{1,0:T(8,128)(2,1)S(1)}, bf16[1024,256]{1,0:T(8,128)(2,1)}, u32[]{:S(2)}) copy-start(bf16[1024,256]{1,0:T(8,128)(2,1)} %do_ref.1) | copy-start | bytes 1572868
  3.8 0.9 %copy-start.3 = (bf16[1024,128]{1,0:T(8,128)(2,1)S(1)}, bf16[1024,128]{1,0:T(8,128)(2,1)}, u32[]{:S(2)}) copy-start(bf16[1024,128]{1,0:T(8,128)(2,1)} %kv_ref.1) | copy-start | bytes 786436
  4.7 0.7 copy-start.4
  5.4 0.7 copy-start.5
  6.1 0.7 copy-start.6

commit v2 on v1

v2 whole, which is shorter than its diff:
```python
import functools

import jax
import jax.numpy as jnp
from jax import lax
from jax.experimental import pallas as pl
from jax.experimental.pallas import tpu as pltpu
from jax.sharding import PartitionSpec as P

HD = 64
QH = 4
BLK = 512
BPD = 2
SPAN = 3
ROWS = BPD * BLK
HALF = 256
NCH = 8
LOG2E = 1.4426950408889634
SCALE = HD**-0.5
DEAD = 1e30
MESH = pl.DeviceIdType.MESH
F32 = jnp.float32
BF16 = jnp.bfloat16


def nt(a, b):
    return lax.dot_general(a, b, (((1,), (1,)), ((), ())), preferred_element_type=F32)


def nn(a, b):
    return lax.dot_general(a, b, (((1,), (0,)), ((), ())), preferred_element_type=F32)


def pick(cond, a, b):
    return lax.select(jnp.broadcast_to(cond, a.shape), a, b)


def kernel(
    n,
    q_ref, o_ref, do_ref, lse_ref, kv_ref, holding_ref, mask_ref,
    dq_ref, dkv_ref,
    qv, ov, dov, lsev, kvw, ktw, packed, sendb, recvb, stat_send, stat_pool, lsew, deltaw, wbuf,
    acc, dqt, dqo, dkv_send, dkv_in, dkv_out,
    load_sem, out_sem, send_sem, recv_sem,
):
    me = lax.axis_index("blk")
    nxt = lax.rem(me + 1, n)
    prv = lax.rem(me + n - 1, n)

    barrier = pltpu.get_barrier_semaphore()
    for dev in (prv, nxt):
        pl.semaphore_signal(barrier, inc=1, device_id={"blk": dev}, device_id_type=MESH)

    loads, load_outs = [], []
    for p in range(2):
        cols = pl.ds(p * 128, 128)
        loads.append(pltpu.make_async_copy(q_ref.at[:, cols], qv.at[p], load_sem.at[3 * p]))
        loads.append(pltpu.make_async_copy(do_ref.at[:, cols], dov.at[p], load_sem.at[3 * p + 1]))
        load_outs.append(pltpu.make_async_copy(o_ref.at[:, cols], ov.at[p], load_sem.at[3 * p + 2]))
    load_lse = pltpu.make_async_copy(lse_ref, lsev, load_sem.at[6])
    load_kv = pltpu.make_async_copy(kv_ref, kvw.at[pl.ds(ROWS, ROWS)], load_sem.at[7])
    for c in loads:
        c.start()
    load_kv.start()
    load_lse.start()
    for c in load_outs:
        c.start()

    def remote(src, dst, idx, dev):
        return pltpu.make_async_remote_copy(
            src_ref=src, dst_ref=dst, send_sem=send_sem.at[idx], recv_sem=recv_sem.at[idx],
            device_id={"blk": dev}, device_id_type=MESH,
        )

    kv_copy = remote(kvw.at[pl.ds(ROWS, ROWS)], kvw.at[pl.ds(0, ROWS)], 0, nxt)
    stat_copies = [
        remote(stat_send.at[0], stat_pool.at[2], 1, nxt),
        remote(stat_send.at[1], stat_pool.at[3], 2, prv),
    ]
    dkv_copies = [
        remote(dkv_send.at[pl.ds(i * BLK, BLK)], dkv_in.at[pl.ds(i * BLK, BLK)], 3 + i, prv)
        for i in range(BPD)
    ]

    def row_copy(j, side):
        return remote(sendb.at[side, j], recvb.at[side, j], 5 + 2 * j + side, nxt if side == 0 else prv)

    h0 = holding_ref[2 * me]
    h1 = holding_ref[2 * me + 1]
    p0 = holding_ref[2 * prv]
    p1 = holding_ref[2 * prv + 1]
    second = [(h1 >> 1) == me + 1, (h1 >> 1) == me - 1]
    low = lax.broadcasted_iota(jnp.int32, (HALF, 128), 1) < HD

    def pack(t, p):
        for slot in range(BPD):
            r = pl.ds(slot * BLK + t * HALF, HALF)
            qf = qv[p, r, :].astype(F32)
            df = dov[p, r, :].astype(F32)
            j = 4 * (1 - t) + 2 * p
            packed[slot, j] = jnp.where(low, qf, pltpu.roll(df, HD, 1)).astype(BF16)
            packed[slot, j + 1] = jnp.where(low, pltpu.roll(qf, HD, 1), df).astype(BF16)
        for j in (j, j + 1):
            for side in range(2):
                sendb[side, j] = pick(second[side], packed[1, j], packed[0, j])

    for c in loads[:2]:
        c.wait()
    pack(1, 0)
    pl.semaphore_wait(barrier, 2)
    for j in range(2):
        for side in range(2):
            row_copy(j, side).start()
    load_kv.wait()
    kv_copy.start()

    for c in loads[2:]:
        c.wait()
    load_lse.wait()
    for c in load_outs:
        c.wait()
    head_of = lax.broadcasted_iota(jnp.int32, (8, 128), 1) // HD
    row_of = lax.broadcasted_iota(jnp.int32, (8, 128), 0)
    delta = jnp.zeros((8, ROWS), F32)
    for p in range(2):
        prod = ov[p].astype(F32) * dov[p].astype(F32)
        hi = prod.astype(BF16)
        lo = (prod - hi.astype(F32)).astype(BF16)
        ind = (row_of == head_of + 4 + 2 * p).astype(BF16)
        delta = delta + nt(ind, hi) + nt(ind, lo)
    for slot in range(BPD):
        cols = pl.ds(slot * BLK, BLK)
        stat_pool[slot, 4:8, :] = delta[4:8, slot * BLK : (slot + 1) * BLK]
        stat_pool[slot, 0:4, :] = lsev[:, cols] * LOG2E
    for side in range(2):
        stat_send[side] = pick(second[side], stat_pool[1], stat_pool[0])
        stat_copies[side].start()

    pack(1, 1)
    pack(0, 0)
    pack(0, 1)

    def transpose_keys(base):
        for i in range(ROWS // HALF):
            kt = kvw[pl.ds(base + i * HALF, HALF), :].astype(F32).T
            ktw[:, pl.ds(base + i * HALF, HALF)] = kt[:HD].astype(BF16)

    transpose_keys(ROWS)
    acc[...] = jnp.zeros_like(acc)

    for c in stat_copies:
        c.wait_recv()
    is0, is1, isp = [], [], []
    for s in range(BPD):
        b = BPD * me + s
        is0.append(h0 == b)
        is1.append(h1 == b)
        isp.append((p0 == b) | (p1 == b))

    def choose(s, own0, own1, before, after):
        return pick(is0[s], own0, pick(is1[s], own1, pick(isp[s], before, after)))

    for s in range(BPD):
        st = choose(s, stat_pool[0], stat_pool[1], stat_pool[2], stat_pool[3])
        for w in range(SPAN):
            alive = (mask_ref[s, w] == 1) & (BPD * me + s >= w)
            bias = jnp.where(alive, 0.0, DEAD).astype(F32)
            lw = st + bias
            for h in range(QH):
                for t in range(2):
                    lsew[s, w, t, h] = lw[h : h + 1, t * HALF : (t + 1) * HALF]
        for h in range(QH):
            for t in range(2):
                deltaw[s, t, h] = st[4 + h : 5 + h, t * HALF : (t + 1) * HALF]

    kv_copy.wait_recv()
    transpose_keys(0)

    causal = lax.broadcasted_iota(jnp.int32, (HALF, HALF), 0) <= lax.broadcasted_iota(
        jnp.int32, (HALF, HALF), 1
    )
    low_half = low[:1].astype(BF16)
    high_half = (~low[:1]).astype(BF16)

    def attend(t, h, s, base, segments, first):
        size = sum(seg[0] for seg in segments)
        rows = pl.ds(base, size)
        j = 4 * (1 - t) + h
        w1 = wbuf[j, s, 0]
        w2 = wbuf[j, s, 1]
        kv = kvw[rows, :]
        scores = nt(kv, w1)
        prob_grads = nt(kv, w2)
        dlt = deltaw[s, t, h]
        probs, grads = [], []
        at = 0
        for count, w, masked in segments:
            pr = jnp.exp2(scores[at : at + count] * (SCALE * LOG2E) - lsew[s, w, t, h])
            if masked:
                pr = jnp.where(causal, pr, 0.0)
            probs.append(pr.astype(BF16))
            grads.append((pr * (prob_grads[at : at + count] - dlt)).astype(BF16))
            at += count
        pb = jnp.concatenate(probs, axis=0) if len(probs) > 1 else probs[0]
        gb = jnp.concatenate(grads, axis=0) if len(grads) > 1 else grads[0]
        acc[rows, :] += nn(gb, w1) + nn(pb, w2)
        part = nn(ktw[:, rows], gb)
        cols = pl.ds(pl.multiple_of(h * HD, HD), HD)
        if first:
            dqt[t, s, cols, :] = part
        else:
            dqt[t, s, cols, :] += part

    def prior(t, h):
        attend(t, h, 0, 0, [(BLK, 2, False), (BLK, 1, False)], True)
        attend(t, h, 1, BLK, [(BLK, 2, False)], True)

    def own(t, h):
        diagonal = [(HALF, 0, False)] * t + [(HALF, 0, True)]
        attend(t, h, 0, ROWS, diagonal, False)
        attend(t, h, 1, ROWS, [(BLK, 1, False)] + diagonal, False)

    def arrive(j):
        row_copy(j, 0).wait_recv()
        row_copy(j, 1).wait_recv()

    def weights(j):
        for s in range(BPD):
            x = choose(s, packed[0, j], packed[1, j], recvb[0, j], recvb[1, j])
            wbuf[j, s, 0] = x * low_half
            wbuf[j, s, 1] = x * high_half

    def send_rows(j):
        row_copy(j, 0).start()
        row_copy(j, 1).start()

    def store_queries(t):
        copies = []
        for s in range(BPD):
            r = pl.ds(s * BLK + t * HALF, HALF)
            dqo[r, :] = (dqt[t, s].T * SCALE).astype(BF16)
            c = pltpu.make_async_copy(dqo.at[r], dq_ref.at[r], out_sem.at[2 * t + s])
            c.start()
            copies.append(c)
        return copies

    def later_rows(h, _):
        arrive(h)
        send_rows(h + 2)
        weights(h)
        prior(1, h)
        own(1, h)
        return 0

    lax.fori_loop(0, QH, later_rows, 0)

    def earlier_rows(h, _):
        j = h + QH
        arrive(j)

        @pl.when(j + 2 < NCH)
        def _():
            send_rows(j + 2)

        weights(j)
        prior(0, h)
        return 0

    lax.fori_loop(0, QH, earlier_rows, 0)

    scaled = jnp.where(low[:1], SCALE, 1.0)
    for i in range(BPD):
        r = pl.ds(i * BLK, BLK)
        dkv_send[r, :] = (acc[r, :] * scaled).astype(BF16)
        dkv_copies[i].start()

    stores = store_queries(1)

    def earlier_own(h, _):
        own(0, h)
        return 0

    lax.fori_loop(0, QH, earlier_own, 0)
    stores += store_queries(0)

    for i in range(BPD):
        r = pl.ds(i * BLK, BLK)
        dkv_copies[i].wait_recv()
        mine = acc[pl.ds(ROWS + i * BLK, BLK), :] * scaled
        dkv_out[r, :] = (mine + dkv_in[r, :].astype(F32)).astype(BF16)
        c = pltpu.make_async_copy(dkv_out.at[r], dkv_ref.at[r], out_sem.at[4 + i])
        c.start()
        stores.append(c)

    kv_copy.wait_send()
    for c in stat_copies:
        c.wait_send()
    for j in range(NCH):
        for side in range(2):
            row_copy(j, side).wait_send()
    for c in dkv_copies:
        c.wait_send()
    for c in stores:
        c.wait()


def on_device(n, queries, outputs, out_grads, log_sums, key_values, holding, block_mask):
    hbm = pl.BlockSpec(memory_space=pl.ANY)
    smem = pl.BlockSpec(memory_space=pltpu.SMEM)
    vm = pltpu.VMEM
    return pl.pallas_call(
        functools.partial(kernel, n),
        out_shape=(
            jax.ShapeDtypeStruct((ROWS, QH * HD), BF16),
            jax.ShapeDtypeStruct((ROWS, 2 * HD), BF16),
        ),
        in_specs=[hbm] * 5 + [smem] * 2,
        out_specs=(hbm, hbm),
        scratch_shapes=[
            vm((2, ROWS, 128), BF16),
            vm((2, ROWS, 128), BF16),
            vm((2, ROWS, 128), BF16),
            vm((QH, ROWS), F32),
            vm((2 * ROWS, 128), BF16),
            vm((HD, 2 * ROWS), BF16),
            vm((BPD, NCH, HALF, 128), BF16),
            vm((2, NCH, HALF, 128), BF16),
            vm((2, NCH, HALF, 128), BF16),
            vm((2, 8, BLK), F32),
            vm((4, 8, BLK), F32),
            vm((BPD, SPAN, 2, QH, 1, HALF), F32),
            vm((BPD, 2, QH, 1, HALF), F32),
            vm((NCH, BPD, 2, HALF, 128), BF16),
            vm((2 * ROWS, 128), F32),
            vm((2, BPD, QH * HD, HALF), F32),
            vm((ROWS, QH * HD), BF16),
            vm((ROWS, 128), BF16),
            vm((ROWS, 128), BF16),
            vm((ROWS, 128), BF16),
            pltpu.SemaphoreType.DMA((8,)),
            pltpu.SemaphoreType.DMA((6,)),
            pltpu.SemaphoreType.DMA((21,)),
            pltpu.SemaphoreType.DMA((21,)),
        ],
        compiler_params=pltpu.CompilerParams(
            collective_id=0, has_side_effects=True, vmem_limit_bytes=60 * 1024 * 1024
        ),
    )(queries, outputs, out_grads, log_sums, key_values, holding, block_mask)


def solution(mesh):
    in_specs = (
        P("blk", "head"),
        P("blk", "head"),
        P("blk", "head"),
        P("head", "blk"),
        P("blk", "head"),
        P(),
        P("blk", None),
    )
    out_specs = (P("blk", "head"), P("blk", "head"))
    return jax.shard_map(
        functools.partial(on_device, mesh.shape["blk"]),
        mesh=mesh, in_specs=in_specs, out_specs=out_specs, check_vma=False,
    )
```

time: 84.2 us -> 60.2 us (0.71)
  Pallas kernels: 75.6 us -> 56.7 us
  local copies, waits for them, and re-layouts: 7.61 us -> 2.62 us
    pallas_call x1, Pallas kernels: 75.6 us -> 56.7 us  [on_device(): pl.pallas_call(functools.partial(kernel, n), out_shape=(jax.ShapeDtypeStr...]
    unnamed x16 -> x4, local copies, waits for them, and re-layouts: 7.61 us -> 2.62 us
where the time goes in v2:
time: 60.2 us; the launch traced here: 60 us
  Pallas kernels  56.7 us (94%)
  local copies, waits for them, and re-layouts  2.62 us (4%)
  between operations  0.65 us (1%)
    pallas_call x1, Pallas kernels, on_device(): pl.pallas_call(functools.partial(kernel, n), out_shape=(jax.ShapeDtypeStr...  56.7 us
    unnamed x4, local copies, waits for them, and re-layouts  2.62 us

profile of v2, /device:TPU:16, one launch (start us, length us, event | category | flops | bytes accessed | tf_op | source)
XLA Modules:
  0.0 60.0 jit_solution(14671352251785603371)
XLA Ops:
  0.6 56.7 %shard_map.86 = (bf16[1024,256]{1,0:T(8,128)(2,1)}, bf16[1024,128]{1,0:T(8,128)(2,1)}) custom-call(bf16[1024,256]{1,0:T(8,128)(2,1)} %q_ref.1, bf16[1024,256]{1,0:T(8,128)(2,1)} %o_ref.1, bf16[1024,256]{1,0:T(8,128)(2,1)} %do_ref.1, f32[4,1024]{1,0:T(4,128)} %lse_ref.1, bf16[1024,128]{1,0:T(8,128)(2,1)} %kv_ref.1, s32[128]{0:T(128)} %holding_ref.1, ...), custom_call_target="tpu_custom_call" | custom-call | tf_op jit(solution)/shard_map/pallas_call | solution.py:311
  57.4 0.0 copy-start
  57.4 1.9 %copy.11 = bf16[1024,256]{1,0:T(8,128)(2,1)} copy(bf16[1024,256]{1,0:T(8,128)(2,1)} %get-tuple-element.4) | data formatting | bytes 1048576
  59.3 0.0 copy-done
  59.3 0.7 %copy.12 = bf16[1024,128]{1,0:T(8,128)(2,1)} copy(bf16[1024,128]{1,0:T(8,128)(2,1)S(1)} %copy-done) | data formatting | bytes 524288
Async XLA Ops:
  57.4 1.9 %copy-start = (bf16[1024,128]{1,0:T(8,128)(2,1)S(1)}, bf16[1024,128]{1,0:T(8,128)(2,1)}, u32[]{:S(2)}) copy-start(bf16[1024,128]{1,0:T(8,128)(2,1)} %get-tuple-element.5) | copy-start | bytes 786436

commit v3 on v2

--- a/solution.py
+++ b/solution.py
@@ -15,6 +15,7 @@
 ROWS = BPD * BLK
 HALF = 256
 NCH = 8
+PARTS = 2
 LOG2E = 1.4426950408889634
 SCALE = HD**-0.5
 DEAD = 1e30
@@ -33,6 +34,24 @@
 
 def pick(cond, a, b):
     return lax.select(jnp.broadcast_to(cond, a.shape), a, b)
+
+
+class Copy:
+    def __init__(self, src, dst, sent, landed, to_next, nxt, prv, has_nxt, has_prv):
+        self.args = dict(
+            src_ref=src, dst_ref=dst, send_sem=sent, recv_sem=landed,
+            device_id={"blk": nxt if to_next else prv}, device_id_type=MESH,
+        )
+        self.sends, self.receives = (has_nxt, has_prv) if to_next else (has_prv, has_nxt)
+
+    def start(self):
+        pl.when(self.sends)(lambda: pltpu.make_async_remote_copy(**self.args).start())
+
+    def wait_send(self):
+        pl.when(self.sends)(lambda: pltpu.make_async_remote_copy(**self.args).wait_send())
+
+    def wait_recv(self):
+        pl.when(self.receives)(lambda: pltpu.make_async_remote_copy(**self.args).wait_recv())
 
 
 def kernel(
@@ -47,9 +66,17 @@
     nxt = lax.rem(me + 1, n)
     prv = lax.rem(me + n - 1, n)
 
+    has_prv = me > 0
+    has_nxt = me < n - 1
     barrier = pltpu.get_barrier_semaphore()
-    for dev in (prv, nxt):
-        pl.semaphore_signal(barrier, inc=1, device_id={"blk": dev}, device_id_type=MESH)
+
+    @pl.when(has_prv)
+    def _():
+        pl.semaphore_signal(barrier, inc=1, device_id={"blk": prv}, device_id_type=MESH)
+
+    @pl.when(has_nxt)
+    def _():
+        pl.semaphore_signal(barrier, inc=1, device_id={"blk": nxt}, device_id_type=MESH)
 
     loads, load_outs = [], []
     for p in range(2):
@@ -66,24 +93,21 @@
     for c in load_outs:
         c.start()
 
-    def remote(src, dst, idx, dev):
-        return pltpu.make_async_remote_copy(
-            src_ref=src, dst_ref=dst, send_sem=send_sem.at[idx], recv_sem=recv_sem.at[idx],
-            device_id={"blk": dev}, device_id_type=MESH,
-        )
-
-    kv_copy = remote(kvw.at[pl.ds(ROWS, ROWS)], kvw.at[pl.ds(0, ROWS)], 0, nxt)
+    def remote(src, dst, idx, to_next):
+        return Copy(src, dst, send_sem.at[idx], recv_sem.at[idx], to_next, nxt, prv, has_nxt, has_prv)
+
+    kv_copy = remote(kv_ref, kvw.at[pl.ds(0, ROWS)], 0, True)
     stat_copies = [
-        remote(stat_send.at[0], stat_pool.at[2], 1, nxt),
-        remote(stat_send.at[1], stat_pool.at[3], 2, prv),
+        remote(stat_send.at[0], stat_pool.at[2], 1, True),
+        remote(stat_send.at[1], stat_pool.at[3], 2, False),
     ]
     dkv_copies = [
-        remote(dkv_send.at[pl.ds(i * BLK, BLK)], dkv_in.at[pl.ds(i * BLK, BLK)], 3 + i, prv)
+        remote(dkv_send.at[pl.ds(i * BLK, BLK)], dkv_in.at[pl.ds(i * BLK, BLK)], 3 + i, False)
         for i in range(BPD)
     ]
 
     def row_copy(j, side):
-        return remote(sendb.at[side, j], recvb.at[side, j], 5 + 2 * j + side, nxt if side == 0 else prv)
+        return remote(sendb.at[side, j], recvb.at[side, j], 5 + 2 * j + side, side == 0)
 
     h0 = holding_ref[2 * me]
     h1 = holding_ref[2 * me + 1]
@@ -91,6 +115,10 @@
     p1 = holding_ref[2 * prv + 1]
     second = [(h1 >> 1) == me + 1, (h1 >> 1) == me - 1]
     low = lax.broadcasted_iota(jnp.int32, (HALF, 128), 1) < HD
+
+    def send_rows(j):
+        row_copy(j, 0).start()
+        row_copy(j, 1).start()
 
     def pack(t, p):
         for slot in range(BPD):
@@ -104,15 +132,17 @@
             for side in range(2):
                 sendb[side, j] = pick(second[side], packed[1, j], packed[0, j])
 
+
+    pl.semaphore_wait(barrier, has_prv.astype(jnp.int32) + has_nxt.astype(jnp.int32))
+
+    kv_copy.start()
     for c in loads[:2]:
         c.wait()
     pack(1, 0)
-    pl.semaphore_wait(barrier, 2)
     for j in range(2):
         for side in range(2):
             row_copy(j, side).start()
     load_kv.wait()
-    kv_copy.start()
 
     for c in loads[2:]:
         c.wait()
@@ -137,6 +167,7 @@
         stat_copies[side].start()
 
     pack(1, 1)
+    send_rows(2)
     pack(0, 0)
     pack(0, 1)
 
@@ -174,6 +205,15 @@
                 deltaw[s, t, h] = st[4 + h : 5 + h, t * HALF : (t + 1) * HALF]
 
     kv_copy.wait_recv()
+
+    @pl.when(me == 0)
+    def _():
+        kvw[pl.ds(0, ROWS), :] = jnp.zeros((ROWS, 128), BF16)
+
+    @pl.when(me == n - 1)
+    def _():
+        dkv_in[...] = jnp.zeros_like(dkv_in)
+
     transpose_keys(0)
 
     causal = lax.broadcasted_iota(jnp.int32, (HALF, HALF), 0) <= lax.broadcasted_iota(
@@ -205,7 +245,7 @@
         gb = jnp.concatenate(grads, axis=0) if len(grads) > 1 else grads[0]
         acc[rows, :] += nn(gb, w1) + nn(pb, w2)
         part = nn(ktw[:, rows], gb)
-        cols = pl.ds(pl.multiple_of(h * HD, HD), HD)
+        cols = pl.ds(h * HD if isinstance(h, int) else pl.multiple_of(h * HD, HD), HD)
         if first:
             dqt[t, s, cols, :] = part
         else:
@@ -246,7 +286,7 @@
 
     def later_rows(h, _):
         arrive(h)
-        send_rows(h + 2)
+        send_rows(h + 3)
         weights(h)
         prior(1, h)
         own(1, h)
@@ -258,21 +298,29 @@
         j = h + QH
         arrive(j)
 
-        @pl.when(j + 2 < NCH)
+        @pl.when(j + 3 < NCH)
         def _():
-            send_rows(j + 2)
+            send_rows(j + 3)
 
         weights(j)
         prior(0, h)
         return 0
 
-    lax.fori_loop(0, QH, earlier_rows, 0)
-
+    lax.fori_loop(0, QH - 1, earlier_rows, 0)
+    arrive(NCH - 1)
+    weights(NCH - 1)
     scaled = jnp.where(low[:1], SCALE, 1.0)
-    for i in range(BPD):
+
+    def return_keys(i):
         r = pl.ds(i * BLK, BLK)
         dkv_send[r, :] = (acc[r, :] * scaled).astype(BF16)
         dkv_copies[i].start()
+
+    attend(0, QH - 1, 0, 0, [(BLK, 2, False)], True)
+    return_keys(0)
+    attend(0, QH - 1, 0, BLK, [(BLK, 1, False)], False)
+    attend(0, QH - 1, 1, BLK, [(BLK, 2, False)], True)
+    return_keys(1)
 
     stores = store_queries(1)
 
@@ -304,18 +352,38 @@
         c.wait()
 
 
+def place(dq_in, dkv_in, dq_ref, dkv_ref, dq_v, dkv_v, sem_in, sem_out):
+    steps = []
+    for i in range(PARTS):
+        r = pl.ds(i * (ROWS // PARTS), ROWS // PARTS)
+        for k, (src, mid, dst) in enumerate(((dq_in, dq_v, dq_ref), (dkv_in, dkv_v, dkv_ref))):
+            steps.append(
+                (
+                    pltpu.make_async_copy(src.at[r], mid.at[r], sem_in.at[2 * i + k]),
+                    pltpu.make_async_copy(mid.at[r], dst.at[r], sem_out.at[2 * i + k]),
+                )
+            )
+    for into, _ in steps:
+        into.start()
+    for into, out in steps:
+        into.wait()
+        out.start()
+    for _, out in steps:
+        out.wait()
+
+
 def on_device(n, queries, outputs, out_grads, log_sums, key_values, holding, block_mask):
-    hbm = pl.BlockSpec(memory_space=pl.ANY)
+    hbm = pl.BlockSpec(memory_space=pltpu.HBM)
     smem = pl.BlockSpec(memory_space=pltpu.SMEM)
     vm = pltpu.VMEM
-    return pl.pallas_call(
+    dq, dkv = pl.pallas_call(
         functools.partial(kernel, n),
         out_shape=(
             jax.ShapeDtypeStruct((ROWS, QH * HD), BF16),
             jax.ShapeDtypeStruct((ROWS, 2 * HD), BF16),
         ),
         in_specs=[hbm] * 5 + [smem] * 2,
-        out_specs=(hbm, hbm),
+        out_specs=(pl.BlockSpec(memory_space=pl.ANY),) * 2,
         scratch_shapes=[
             vm((2, ROWS, 128), BF16),
             vm((2, ROWS, 128), BF16),
@@ -346,6 +414,22 @@
             collective_id=0, has_side_effects=True, vmem_limit_bytes=60 * 1024 * 1024
         ),
     )(queries, outputs, out_grads, log_sums, key_values, holding, block_mask)
+    return pl.pallas_call(
+        place,
+        out_shape=(
+            jax.ShapeDtypeStruct((ROWS, QH * HD), BF16),
+            jax.ShapeDtypeStruct((ROWS, 2 * HD), BF16),
+        ),
+        in_specs=[hbm] * 2,
+        out_specs=(pl.BlockSpec(memory_space=pl.ANY),) * 2,
+        scratch_shapes=[
+            vm((ROWS, QH * HD), BF16),
+            vm((ROWS, 2 * HD), BF16),
+            pltpu.SemaphoreType.DMA((2 * PARTS,)),
+            pltpu.SemaphoreType.DMA((2 * PARTS,)),
+        ],
+        compiler_params=pltpu.CompilerParams(vmem_limit_bytes=60 * 1024 * 1024),
+    )(dq, dkv)
 
 
 def solution(mesh):

time: 60.2 us -> 49.8 us (0.83)
  the two profiles are of different devices: /device:TPU:16 before, /device:TPU:254 now
where the time goes in v3:
time: 49.8 us; the launch traced here: 49.6 us
  Pallas kernels  49 us (98%)
  between operations  0.64 us (1%)
    pallas_call x1, Pallas kernels, on_device(): pl.pallas_call(functools.partial(kernel, n), out_shape=(jax.ShapeDtypeStr...  47.1 us
    pallas_call x1, Pallas kernels, on_device(): pl.pallas_call(place, out_shape=(jax.ShapeDtypeStruct((ROWS, QH * HD), BF...  1.9 us

profile of v3, /device:TPU:254, one launch (start us, length us, event | category | flops | bytes accessed | tf_op | source)
XLA Modules:
  0.0 49.6 jit_solution(17105687757447597883)
XLA Ops:
  0.6 47.1 %shard_map.86 = (bf16[1024,256]{1,0:T(8,128)(2,1)}, bf16[1024,128]{1,0:T(8,128)(2,1)}) custom-call(bf16[1024,256]{1,0:T(8,128)(2,1)} %q_ref.1, bf16[1024,256]{1,0:T(8,128)(2,1)} %o_ref.1, bf16[1024,256]{1,0:T(8,128)(2,1)} %do_ref.1, f32[4,1024]{1,0:T(4,128)} %lse_ref.1, bf16[1024,128]{1,0:T(8,128)(2,1)} %kv_ref.1, s32[128]{0:T(128)} %holding_ref.1, ...), custom_call_target="tpu_custom_call" | custom-call | tf_op jit(solution)/shard_map/pallas_call | solution.py:379
  47.7 1.9 %shard_map.87 = (bf16[1024,256]{1,0:T(8,128)(2,1)}, bf16[1024,128]{1,0:T(8,128)(2,1)}) custom-call(bf16[1024,256]{1,0:T(8,128)(2,1)} %get-tuple-element.4.dq_in, bf16[1024,128]{1,0:T(8,128)(2,1)} %get-tuple-element.5.dkv_in), custom_call_target="tpu_custom_call" | custom-call | tf_op jit(solution)/shard_map/pallas_call | solution.py:417

commit v4 on v3

--- a/solution.py
+++ b/solution.py
@@ -15,7 +15,6 @@
 ROWS = BPD * BLK
 HALF = 256
 NCH = 8
-PARTS = 2
 LOG2E = 1.4426950408889634
 SCALE = HD**-0.5
 DEAD = 1e30
@@ -57,9 +56,9 @@
 def kernel(
     n,
     q_ref, o_ref, do_ref, lse_ref, kv_ref, holding_ref, mask_ref,
-    dq_ref, dkv_ref,
+    dq_ref, own_ref, dkv_in,
     qv, ov, dov, lsev, kvw, ktw, packed, sendb, recvb, stat_send, stat_pool, lsew, deltaw, wbuf,
-    acc, dqt, dqo, dkv_send, dkv_in, dkv_out,
+    acc, dqt, dqo, dkv_send, zeros,
     load_sem, out_sem, send_sem, recv_sem,
 ):
     me = lax.axis_index("blk")
@@ -168,8 +167,13 @@
 
     pack(1, 1)
     send_rows(2)
+    send_rows(3)
     pack(0, 0)
+    send_rows(4)
+    send_rows(5)
     pack(0, 1)
+    send_rows(6)
+    send_rows(7)
 
     def transpose_keys(base):
         for i in range(ROWS // HALF):
@@ -212,7 +216,10 @@
 
     @pl.when(me == n - 1)
     def _():
-        dkv_in[...] = jnp.zeros_like(dkv_in)
+        zeros[...] = jnp.zeros_like(zeros)
+        fill = pltpu.make_async_copy(zeros, dkv_in, out_sem.at[5])
+        fill.start()
+        fill.wait()
 
     transpose_keys(0)
 
@@ -286,7 +293,6 @@
 
     def later_rows(h, _):
         arrive(h)
-        send_rows(h + 3)
         weights(h)
         prior(1, h)
         own(1, h)
@@ -297,10 +303,6 @@
     def earlier_rows(h, _):
         j = h + QH
         arrive(j)
-
-        @pl.when(j + 3 < NCH)
-        def _():
-            send_rows(j + 3)
 
         weights(j)
         prior(0, h)
@@ -330,15 +332,12 @@
 
     lax.fori_loop(0, QH, earlier_own, 0)
     stores += store_queries(0)
-
-    for i in range(BPD):
-        r = pl.ds(i * BLK, BLK)
-        dkv_copies[i].wait_recv()
-        mine = acc[pl.ds(ROWS + i * BLK, BLK), :] * scaled
-        dkv_out[r, :] = (mine + dkv_in[r, :].astype(F32)).astype(BF16)
-        c = pltpu.make_async_copy(dkv_out.at[r], dkv_ref.at[r], out_sem.at[4 + i])
-        c.start()
-        stores.append(c)
+    c = pltpu.make_async_copy(acc.at[pl.ds(ROWS, ROWS)], own_ref, out_sem.at[4])
+    c.start()
+    stores.append(c)
+
+    for c in dkv_copies:
+        c.wait_recv()
 
     kv_copy.wait_send()
     for c in stat_copies:
@@ -352,38 +351,42 @@
         c.wait()
 
 
-def place(dq_in, dkv_in, dq_ref, dkv_ref, dq_v, dkv_v, sem_in, sem_out):
-    steps = []
-    for i in range(PARTS):
-        r = pl.ds(i * (ROWS // PARTS), ROWS // PARTS)
-        for k, (src, mid, dst) in enumerate(((dq_in, dq_v, dq_ref), (dkv_in, dkv_v, dkv_ref))):
-            steps.append(
-                (
-                    pltpu.make_async_copy(src.at[r], mid.at[r], sem_in.at[2 * i + k]),
-                    pltpu.make_async_copy(mid.at[r], dst.at[r], sem_out.at[2 * i + k]),
-                )
-            )
-    for into, _ in steps:
-        into.start()
-    for into, out in steps:
-        into.wait()
-        out.start()
-    for _, out in steps:
-        out.wait()
+def finish(dq_in, own, theirs, dq_ref, dkv_ref, dq_v, own_v, theirs_v, sem_in, sem_out):
+    half = [pl.ds(i * BLK, BLK) for i in range(BPD)]
+    into = []
+    for i, r in enumerate(half):
+        for k, (src, dst) in enumerate(((own, own_v), (theirs, theirs_v), (dq_in, dq_v))):
+            into.append(pltpu.make_async_copy(src.at[r], dst.at[r], sem_in.at[3 * i + k]))
+    for c in into:
+        c.start()
+    scaled = jnp.where(lax.broadcasted_iota(jnp.int32, (1, 128), 1) < HD, SCALE, 1.0)
+    out = []
+    for i, r in enumerate(half):
+        into[3 * i].wait()
+        into[3 * i + 1].wait()
+        theirs_v[r, :] = (own_v[r, :] * scaled + theirs_v[r, :].astype(F32)).astype(BF16)
+        out.append(pltpu.make_async_copy(theirs_v.at[r], dkv_ref.at[r], sem_out.at[2 * i]))
+        out[-1].start()
+        into[3 * i + 2].wait()
+        out.append(pltpu.make_async_copy(dq_v.at[r], dq_ref.at[r], sem_out.at[2 * i + 1]))
+        out[-1].start()
+    for c in out:
+        c.wait()
 
 
 def on_device(n, queries, outputs, out_grads, log_sums, key_values, holding, block_mask):
     hbm = pl.BlockSpec(memory_space=pltpu.HBM)
     smem = pl.BlockSpec(memory_space=pltpu.SMEM)
     vm = pltpu.VMEM
-    dq, dkv = pl.pallas_call(
+    dq, mine, theirs = pl.pallas_call(
         functools.partial(kernel, n),
         out_shape=(
             jax.ShapeDtypeStruct((ROWS, QH * HD), BF16),
+            jax.ShapeDtypeStruct((ROWS, 2 * HD), F32),
             jax.ShapeDtypeStruct((ROWS, 2 * HD), BF16),
         ),
         in_specs=[hbm] * 5 + [smem] * 2,
-        out_specs=(pl.BlockSpec(memory_space=pl.ANY),) * 2,
+        out_specs=(pl.BlockSpec(memory_space=pl.ANY),) * 3,
         scratch_shapes=[
             vm((2, ROWS, 128), BF16),
             vm((2, ROWS, 128), BF16),
@@ -404,7 +407,6 @@
             vm((ROWS, QH * HD), BF16),
             vm((ROWS, 128), BF16),
             vm((ROWS, 128), BF16),
-            vm((ROWS, 128), BF16),
             pltpu.SemaphoreType.DMA((8,)),
             pltpu.SemaphoreType.DMA((6,)),
             pltpu.SemaphoreType.DMA((21,)),
@@ -415,21 +417,22 @@
         ),
     )(queries, outputs, out_grads, log_sums, key_values, holding, block_mask)
     return pl.pallas_call(
-        place,
+        finish,
         out_shape=(
             jax.ShapeDtypeStruct((ROWS, QH * HD), BF16),
             jax.ShapeDtypeStruct((ROWS, 2 * HD), BF16),
         ),
-        in_specs=[hbm] * 2,
+        in_specs=[hbm] * 3,
         out_specs=(pl.BlockSpec(memory_space=pl.ANY),) * 2,
         scratch_shapes=[
             vm((ROWS, QH * HD), BF16),
+            vm((ROWS, 2 * HD), F32),
             vm((ROWS, 2 * HD), BF16),
-            pltpu.SemaphoreType.DMA((2 * PARTS,)),
-            pltpu.SemaphoreType.DMA((2 * PARTS,)),
+            pltpu.SemaphoreType.DMA((6,)),
+            pltpu.SemaphoreType.DMA((4,)),
         ],
         compiler_params=pltpu.CompilerParams(vmem_limit_bytes=60 * 1024 * 1024),
-    )(dq, dkv)
+    )(dq, mine, theirs)
 
 
 def solution(mesh):

time: 49.8 us -> 49.2 us (0.988)
  Pallas kernels: 49 us -> 48.4 us
    pallas_call x1, Pallas kernels: 47.1 us -> 46.3 us  [on_device(): pl.pallas_call(functools.partial(kernel, n), out_shape=(jax.ShapeDtypeStr...]
where the time goes in v4:
time: 49.2 us; the launch traced here: 49 us
  Pallas kernels  48.4 us (98%)
  between operations  0.64 us (1%)
    pallas_call x1, Pallas kernels, on_device(): pl.pallas_call(functools.partial(kernel, n), out_shape=(jax.ShapeDtypeStr...  46.3 us
    pallas_call x1, Pallas kernels, on_device(): pl.pallas_call(finish, out_shape=(jax.ShapeDtypeStruct((ROWS, QH * HD), B...  2.08 us

profile of v4, /device:TPU:254, one launch (start us, length us, event | category | flops | bytes accessed | tf_op | source)
XLA Modules:
  0.0 49.0 jit_solution(2753256392166868823)
XLA Ops:
  0.6 46.3 %shard_map.86 = (bf16[1024,256]{1,0:T(8,128)(2,1)}, f32[1024,128]{1,0:T(8,128)}, bf16[1024,128]{1,0:T(8,128)(2,1)}) custom-call(bf16[1024,256]{1,0:T(8,128)(2,1)} %q_ref.1, bf16[1024,256]{1,0:T(8,128)(2,1)} %o_ref.1, bf16[1024,256]{1,0:T(8,128)(2,1)} %do_ref.1, f32[4,1024]{1,0:T(4,128)} %lse_ref.1, bf16[1024,128]{1,0:T(8,128)(2,1)} %kv_ref.1, ...), custom_call_target="tpu_custom_call" | custom-call | tf_op jit(solution)/shard_map/pallas_call | solution.py:381
  46.9 2.1 %shard_map.87 = (bf16[1024,256]{1,0:T(8,128)(2,1)}, bf16[1024,128]{1,0:T(8,128)(2,1)}) custom-call(bf16[1024,256]{1,0:T(8,128)(2,1)} %get-tuple-element.5.dq_in, f32[1024,128]{1,0:T(8,128)} %get-tuple-element.6.own, bf16[1024,128]{1,0:T(8,128)(2,1)} %get-tuple-element.7.theirs), custom_call_target="tpu_custom_call" | custom-call | tf_op jit(solution)/shard_map/pallas_call | solution.py:419

commit v5 on v4

--- a/solution.py
+++ b/solution.py
@@ -55,11 +55,12 @@
 
 def kernel(
     n,
-    q_ref, o_ref, do_ref, lse_ref, kv_ref, holding_ref, mask_ref,
+    q_ref, o_ref, do_ref, lse_ref, kv_ref, holding_hbm, mask_hbm,
     dq_ref, own_ref, dkv_in,
     qv, ov, dov, lsev, kvw, ktw, packed, sendb, recvb, stat_send, stat_pool, lsew, deltaw, wbuf,
-    acc, dqt, dqo, dkv_send, zeros,
-    load_sem, out_sem, send_sem, recv_sem,
+    acc, dqt, dkv_send, holding_ref, mask_ref,
+
+    load_sem, send_sem, recv_sem,
 ):
     me = lax.axis_index("blk")
     nxt = lax.rem(me + 1, n)
@@ -85,7 +86,11 @@
         load_outs.append(pltpu.make_async_copy(o_ref.at[:, cols], ov.at[p], load_sem.at[3 * p + 2]))
     load_lse = pltpu.make_async_copy(lse_ref, lsev, load_sem.at[6])
     load_kv = pltpu.make_async_copy(kv_ref, kvw.at[pl.ds(ROWS, ROWS)], load_sem.at[7])
-    for c in loads:
+    small = [
+        pltpu.make_async_copy(holding_hbm, holding_ref, load_sem.at[8]),
+        pltpu.make_async_copy(mask_hbm, mask_ref, load_sem.at[9]),
+    ]
+    for c in small + loads:
         c.start()
     load_kv.start()
     load_lse.start()
@@ -108,11 +113,6 @@
     def row_copy(j, side):
         return remote(sendb.at[side, j], recvb.at[side, j], 5 + 2 * j + side, side == 0)
 
-    h0 = holding_ref[2 * me]
-    h1 = holding_ref[2 * me + 1]
-    p0 = holding_ref[2 * prv]
-    p1 = holding_ref[2 * prv + 1]
-    second = [(h1 >> 1) == me + 1, (h1 >> 1) == me - 1]
     low = lax.broadcasted_iota(jnp.int32, (HALF, 128), 1) < HD
 
     def send_rows(j):
@@ -135,6 +135,13 @@
     pl.semaphore_wait(barrier, has_prv.astype(jnp.int32) + has_nxt.astype(jnp.int32))
 
     kv_copy.start()
+    for c in small:
+        c.wait()
+    h0 = holding_ref[2 * me]
+    h1 = holding_ref[2 * me + 1]
+    p0 = holding_ref[2 * prv]
+    p1 = holding_ref[2 * prv + 1]
+    second = [(h1 >> 1) == me + 1, (h1 >> 1) == me - 1]
     for c in loads[:2]:
         c.wait()
     pack(1, 0)
@@ -216,10 +223,7 @@
 
     @pl.when(me == n - 1)
     def _():
-        zeros[...] = jnp.zeros_like(zeros)
-        fill = pltpu.make_async_copy(zeros, dkv_in, out_sem.at[5])
-        fill.start()
-        fill.wait()
+        dkv_in[...] = jnp.zeros_like(dkv_in)
 
     transpose_keys(0)
 
@@ -282,14 +286,9 @@
         row_copy(j, 1).start()
 
     def store_queries(t):
-        copies = []
         for s in range(BPD):
             r = pl.ds(s * BLK + t * HALF, HALF)
-            dqo[r, :] = (dqt[t, s].T * SCALE).astype(BF16)
-            c = pltpu.make_async_copy(dqo.at[r], dq_ref.at[r], out_sem.at[2 * t + s])
-            c.start()
-            copies.append(c)
-        return copies
+            dq_ref[r, :] = (dqt[t, s].T * SCALE).astype(BF16)
 
     def later_rows(h, _):
         arrive(h)
@@ -324,17 +323,15 @@
     attend(0, QH - 1, 1, BLK, [(BLK, 2, False)], True)
     return_keys(1)
 
-    stores = store_queries(1)
+    store_queries(1)
 
     def earlier_own(h, _):
         own(0, h)
         return 0
 
     lax.fori_loop(0, QH, earlier_own, 0)
-    stores += store_queries(0)
-    c = pltpu.make_async_copy(acc.at[pl.ds(ROWS, ROWS)], own_ref, out_sem.at[4])
-    c.start()
-    stores.append(c)
+    store_queries(0)
+    own_ref[...] = acc[pl.ds(ROWS, ROWS), :] * scaled
 
     for c in dkv_copies:
         c.wait_recv()
@@ -347,28 +344,15 @@
             row_copy(j, side).wait_send()
     for c in dkv_copies:
         c.wait_send()
-    for c in stores:
-        c.wait()
-
-
-def finish(dq_in, own, theirs, dq_ref, dkv_ref, dq_v, own_v, theirs_v, sem_in, sem_out):
-    half = [pl.ds(i * BLK, BLK) for i in range(BPD)]
-    into = []
-    for i, r in enumerate(half):
-        for k, (src, dst) in enumerate(((own, own_v), (theirs, theirs_v), (dq_in, dq_v))):
-            into.append(pltpu.make_async_copy(src.at[r], dst.at[r], sem_in.at[3 * i + k]))
-    for c in into:
-        c.start()
-    scaled = jnp.where(lax.broadcasted_iota(jnp.int32, (1, 128), 1) < HD, SCALE, 1.0)
-    out = []
-    for i, r in enumerate(half):
-        into[3 * i].wait()
-        into[3 * i + 1].wait()
-        theirs_v[r, :] = (own_v[r, :] * scaled + theirs_v[r, :].astype(F32)).astype(BF16)
-        out.append(pltpu.make_async_copy(theirs_v.at[r], dkv_ref.at[r], sem_out.at[2 * i]))
-        out[-1].start()
-        into[3 * i + 2].wait()
-        out.append(pltpu.make_async_copy(dq_v.at[r], dq_ref.at[r], sem_out.at[2 * i + 1]))
+
+
+def finish(dq_in, own, theirs, dq_ref, dkv_ref, total, sem):
+    out = [pltpu.make_async_copy(dq_in, dq_ref, sem.at[0])]
+    out[0].start()
+    for i in range(BPD):
+        r = pl.ds(i * BLK, BLK)
+        total[r, :] = (own[r, :] + theirs[r, :].astype(F32)).astype(BF16)
+        out.append(pltpu.make_async_copy(total.at[r], dkv_ref.at[r], sem.at[1 + i]))
         out[-1].start()
     for c in out:
         c.wait()
@@ -376,17 +360,16 @@
 
 def on_device(n, queries, outputs, out_grads, log_sums, key_values, holding, block_mask):
     hbm = pl.BlockSpec(memory_space=pltpu.HBM)
-    smem = pl.BlockSpec(memory_space=pltpu.SMEM)
     vm = pltpu.VMEM
     dq, mine, theirs = pl.pallas_call(
         functools.partial(kernel, n),
         out_shape=(
-            jax.ShapeDtypeStruct((ROWS, QH * HD), BF16),
-            jax.ShapeDtypeStruct((ROWS, 2 * HD), F32),
-            jax.ShapeDtypeStruct((ROWS, 2 * HD), BF16),
+            vm((ROWS, QH * HD), BF16),
+            vm((ROWS, 2 * HD), F32),
+            vm((ROWS, 2 * HD), BF16),
         ),
-        in_specs=[hbm] * 5 + [smem] * 2,
-        out_specs=(pl.BlockSpec(memory_space=pl.ANY),) * 3,
+        in_specs=[hbm] * 7,
+        out_specs=(pl.BlockSpec(memory_space=pltpu.VMEM),) * 3,
         scratch_shapes=[
             vm((2, ROWS, 128), BF16),
             vm((2, ROWS, 128), BF16),
@@ -404,35 +387,33 @@
             vm((NCH, BPD, 2, HALF, 128), BF16),
             vm((2 * ROWS, 128), F32),
             vm((2, BPD, QH * HD, HALF), F32),
-            vm((ROWS, QH * HD), BF16),
             vm((ROWS, 128), BF16),
-            vm((ROWS, 128), BF16),
-            pltpu.SemaphoreType.DMA((8,)),
-            pltpu.SemaphoreType.DMA((6,)),
+            pltpu.SMEM((holding.shape[0],), jnp.int32),
+            pltpu.SMEM((BPD, SPAN), jnp.int32),
+            pltpu.SemaphoreType.DMA((10,)),
             pltpu.SemaphoreType.DMA((21,)),
             pltpu.SemaphoreType.DMA((21,)),
         ],
         compiler_params=pltpu.CompilerParams(
-            collective_id=0, has_side_effects=True, vmem_limit_bytes=60 * 1024 * 1024
+            collective_id=0, has_side_effects=True, vmem_limit_bytes=40 * 1024 * 1024
         ),
-    )(queries, outputs, out_grads, log_sums, key_values, holding, block_mask)
+    )(
+        *(
+            pltpu.with_memory_space_constraint(x, pltpu.HBM)
+            for x in (queries, outputs, out_grads, log_sums, key_values, holding, block_mask)
+        )
+    )
     return pl.pallas_call(
         finish,
         out_shape=(
             jax.ShapeDtypeStruct((ROWS, QH * HD), BF16),
             jax.ShapeDtypeStruct((ROWS, 2 * HD), BF16),
         ),
-        in_specs=[hbm] * 3,
+        in_specs=[pl.BlockSpec(memory_space=pltpu.VMEM)] * 3,
         out_specs=(pl.BlockSpec(memory_space=pl.ANY),) * 2,
-        scratch_shapes=[
-            vm((ROWS, QH * HD), BF16),
-            vm((ROWS, 2 * HD), F32),
-            vm((ROWS, 2 * HD), BF16),
-            pltpu.SemaphoreType.DMA((6,)),
-            pltpu.SemaphoreType.DMA((4,)),
-        ],
-        compiler_params=pltpu.CompilerParams(vmem_limit_bytes=60 * 1024 * 1024),
-    )(dq, mine, theirs)
+        scratch_shapes=[vm((ROWS, 2 * HD), BF16), pltpu.SemaphoreType.DMA((1 + BPD,))],
+        compiler_params=pltpu.CompilerParams(vmem_limit_bytes=40 * 1024 * 1024),
+    )(*(pltpu.with_memory_space_constraint(x, pltpu.VMEM) for x in (dq, mine, theirs)))
 
 
 def solution(mesh):

time: 49.2 us -> 47.1 us (0.957)
  Pallas kernels: 48.4 us -> 46.3 us
    pallas_call x1, Pallas kernels: 2.08 us -> 0.9 us  [on_device(): pl.pallas_call(finish, out_shape=(jax.ShapeDtypeStruct((ROWS, QH * HD), B...]
    pallas_call x1, Pallas kernels: 46.3 us -> 45.4 us  [on_device(): pl.pallas_call(functools.partial(kernel, n), out_shape=(vm((ROWS, QH * HD...]
where the time goes in v5:
time: 47.1 us; the launch traced here: 47 us
  Pallas kernels  46.3 us (98%)
  between operations  0.64 us (1%)
    pallas_call x1, Pallas kernels, on_device(): pl.pallas_call(functools.partial(kernel, n), out_shape=(vm((ROWS, QH * HD...  45.4 us

profile of v5, /device:TPU:254, one launch (start us, length us, event | category | flops | bytes accessed | tf_op | source)
XLA Modules:
  0.0 47.0 jit_solution(6329508799992262423)
XLA Ops:
  0.6 45.4 %shard_map.86 = (bf16[1024,256]{1,0:T(8,128)(2,1)S(1)}, f32[1024,128]{1,0:T(8,128)S(1)}, bf16[1024,128]{1,0:T(8,128)(2,1)S(1)}) custom-call(bf16[1024,256]{1,0:T(8,128)(2,1)} %q_ref.1, bf16[1024,256]{1,0:T(8,128)(2,1)} %o_ref.1, bf16[1024,256]{1,0:T(8,128)(2,1)} %do_ref.1, f32[4,1024]{1,0:T(4,128)} %lse_ref.1, bf16[1024,128]{1,0:T(8,128)(2,1)} %kv_ref.1, ...), custom_call_target="tpu_custom_call" | custom-call | tf_op jit(solution)/shard_map/pallas_call | solution.py:364
  46.1 0.9 %shard_map.87 = (bf16[1024,256]{1,0:T(8,128)(2,1)}, bf16[1024,128]{1,0:T(8,128)(2,1)}) custom-call(bf16[1024,256]{1,0:T(8,128)(2,1)S(1)} %get-tuple-element.5.dq_in, f32[1024,128]{1,0:T(8,128)S(1)} %get-tuple-element.6.own, bf16[1024,128]{1,0:T(8,128)(2,1)S(1)} %get-tuple-element.7.theirs), custom_call_target="tpu_custom_call" | custom-call | tf_op jit(solution)/shard_map/pallas_call | solution.py:406

commit v6 on v5

--- a/solution.py
+++ b/solution.py
@@ -333,9 +333,6 @@
     store_queries(0)
     own_ref[...] = acc[pl.ds(ROWS, ROWS), :] * scaled
 
-    for c in dkv_copies:
-        c.wait_recv()
-
     kv_copy.wait_send()
     for c in stat_copies:
         c.wait_send()
@@ -344,6 +341,8 @@
             row_copy(j, side).wait_send()
     for c in dkv_copies:
         c.wait_send()
+    for c in dkv_copies:
+        c.wait_recv()
 
 
 def finish(dq_in, own, theirs, dq_ref, dkv_ref, total, sem):

time: 47.1 us -> 47.1 us (level)
  no operation moved by 1% of the time
where the time goes in v6:
time: 47.1 us; the launch traced here: 47 us
  Pallas kernels  46.3 us (98%)
  between operations  0.64 us (1%)
    pallas_call x1, Pallas kernels, on_device(): pl.pallas_call(functools.partial(kernel, n), out_shape=(vm((ROWS, QH * HD...  45.4 us

profile of v6, /device:TPU:254, one launch (start us, length us, event | category | flops | bytes accessed | tf_op | source)
XLA Modules:
  0.0 47.0 jit_solution(14844774599749358881)
XLA Ops:
  0.6 45.4 %shard_map.86 = (bf16[1024,256]{1,0:T(8,128)(2,1)S(1)}, f32[1024,128]{1,0:T(8,128)S(1)}, bf16[1024,128]{1,0:T(8,128)(2,1)S(1)}) custom-call(bf16[1024,256]{1,0:T(8,128)(2,1)} %q_ref.1, bf16[1024,256]{1,0:T(8,128)(2,1)} %o_ref.1, bf16[1024,256]{1,0:T(8,128)(2,1)} %do_ref.1, f32[4,1024]{1,0:T(4,128)} %lse_ref.1, bf16[1024,128]{1,0:T(8,128)(2,1)} %kv_ref.1, ...), custom_call_target="tpu_custom_call" | custom-call | tf_op jit(solution)/shard_map/pallas_call | solution.py:363
  46.1 0.9 %shard_map.87 = (bf16[1024,256]{1,0:T(8,128)(2,1)}, bf16[1024,128]{1,0:T(8,128)(2,1)}) custom-call(bf16[1024,256]{1,0:T(8,128)(2,1)S(1)} %get-tuple-element.5.dq_in, f32[1024,128]{1,0:T(8,128)S(1)} %get-tuple-element.6.own, bf16[1024,128]{1,0:T(8,128)(2,1)S(1)} %get-tuple-element.7.theirs), custom_call_target="tpu_custom_call" | custom-call | tf_op jit(solution)/shard_map/pallas_call | solution.py:405

commit v7 on v6

--- a/solution.py
+++ b/solution.py
@@ -307,9 +307,7 @@
         prior(0, h)
         return 0
 
-    lax.fori_loop(0, QH - 1, earlier_rows, 0)
-    arrive(NCH - 1)
-    weights(NCH - 1)
+    lax.fori_loop(0, QH - 2, earlier_rows, 0)
     scaled = jnp.where(low[:1], SCALE, 1.0)
 
     def return_keys(i):
@@ -317,10 +315,14 @@
         dkv_send[r, :] = (acc[r, :] * scaled).astype(BF16)
         dkv_copies[i].start()
 
-    attend(0, QH - 1, 0, 0, [(BLK, 2, False)], True)
+    for h in (QH - 2, QH - 1):
+        arrive(QH + h)
+        weights(QH + h)
+        attend(0, h, 0, 0, [(BLK, 2, False)], True)
     return_keys(0)
-    attend(0, QH - 1, 0, BLK, [(BLK, 1, False)], False)
-    attend(0, QH - 1, 1, BLK, [(BLK, 2, False)], True)
+    for h in (QH - 2, QH - 1):
+        attend(0, h, 0, BLK, [(BLK, 1, False)], False)
+        attend(0, h, 1, BLK, [(BLK, 2, False)], True)
     return_keys(1)
 
     store_queries(1)

time: 47.1 us -> 47.2 us (level)
  no operation moved by 1% of the time
where the time goes in v7:
time: 47.2 us; the launch traced here: 47.1 us
  Pallas kernels  46.5 us (99%)
  between operations  0.64 us (1%)
    pallas_call x1, Pallas kernels, on_device(): pl.pallas_call(functools.partial(kernel, n), out_shape=(vm((ROWS, QH * HD...  45.6 us

profile of v7, /device:TPU:254, one launch (start us, length us, event | category | flops | bytes accessed | tf_op | source)
XLA Modules:
  0.0 47.1 jit_solution(11805553697985138299)
XLA Ops:
  0.6 45.6 %shard_map.86 = (bf16[1024,256]{1,0:T(8,128)(2,1)S(1)}, f32[1024,128]{1,0:T(8,128)S(1)}, bf16[1024,128]{1,0:T(8,128)(2,1)S(1)}) custom-call(bf16[1024,256]{1,0:T(8,128)(2,1)} %q_ref.1, bf16[1024,256]{1,0:T(8,128)(2,1)} %o_ref.1, bf16[1024,256]{1,0:T(8,128)(2,1)} %do_ref.1, f32[4,1024]{1,0:T(4,128)} %lse_ref.1, bf16[1024,128]{1,0:T(8,128)(2,1)} %kv_ref.1, ...), custom_call_target="tpu_custom_call" | custom-call | tf_op jit(solution)/shard_map/pallas_call | solution.py:365
  46.2 0.9 %shard_map.87 = (bf16[1024,256]{1,0:T(8,128)(2,1)}, bf16[1024,128]{1,0:T(8,128)(2,1)}) custom-call(bf16[1024,256]{1,0:T(8,128)(2,1)S(1)} %get-tuple-element.5.dq_in, f32[1024,128]{1,0:T(8,128)S(1)} %get-tuple-element.6.own, bf16[1024,128]{1,0:T(8,128)(2,1)S(1)} %get-tuple-element.7.theirs), custom_call_target="tpu_custom_call" | custom-call | tf_op jit(solution)/shard_map/pallas_call | solution.py:407
